TPU v7x, 512 devices: a whole 4x4x16 slice. The times are simulated.
512 devices in a mesh: member: 16 (over y_lo, x, core), space: 32 (over z, y_hi).
Axes of the slice: x: 4, y: 4 (y_hi: 2, y_lo: 2; y = y_hi * 2 + y_lo), z: 16, core: 2. Of those that a mesh axis runs over, the one named last changes fastest.
Arguments:
- depth: float32 [32, 512, 2048], P('member', 'space'), may hold values from 0.05 to 3
- flow_x: float32 [32, 512, 2048], P('member', 'space'), may hold values from -3 to 3
- flow_y: float32 [32, 512, 2048], P('member', 'space'), may hold values from -3 to 3
- terrain: float32 [512, 2048], P('space'), may hold values from -3 to 3
- roughness: float32 [512, 2048], P('space'), may hold values from 0.02 to 0.12
- gauges: int32 [512], replicated, may hold values from 0 to 1048575
- observed: float32 [512], replicated, may hold values from 4 to 6
- ancestors: int32 [32], replicated, may hold values from 0 to 31, as said below
Outputs:
- depth_out: float32 [32, 512, 2048], P('member', 'space')
- flow_x_out: float32 [32, 512, 2048], P('member', 'space')
- flow_y_out: float32 [32, 512, 2048], P('member', 'space')
- log_weight: float32 [32], P('member')
Inputs may be any that keep to these rules, and one draw needn't show every extreme that they name: `ancestors`: each entry names a particle.
All inputs are finite; a program needn't handle non-finite values.
Results may differ from a plain program's by a relative error of at most 0.0003.
Values sent between devices are 32-bit elements; how exact they have to be, the bound alone decides.
A program may use at most 128 MiB of HBM per device.

v0:
```python
import jax
import jax.numpy as jnp
from jax import lax
from jax.sharding import PartitionSpec as P

gravity = 9.81
time_step = 1.0
cell_size = 30.0
depth_floor = 0.1


def padded(block, sides, width):
    for axis, dim in sides:
        count = lax.axis_size(axis)
        forward = [(i, i + 1) for i in range(count - 1)]
        backward = [(target, source) for source, target in forward]
        low = lax.ppermute(
            lax.slice_in_dim(block, block.shape[dim] - width, None, axis=dim), axis, forward
        )
        high = lax.ppermute(lax.slice_in_dim(block, 0, width, axis=dim), axis, backward)
        block = jnp.concatenate([low, block, high], axis=dim)
    return block


def face_flux(flow, eta_a, eta_b, bed_a, bed_b, rough):
    hflow = jnp.maximum(jnp.maximum(eta_a, eta_b) - jnp.maximum(bed_a, bed_b), depth_floor)
    slope = (eta_b - eta_a) / cell_size
    return (flow - gravity * hflow * time_step * slope) / (
        1.0 + gravity * time_step * rough * rough * jnp.abs(flow) / jnp.power(hflow, 7.0 / 3.0)
    )


def with_rims(water, south):
    return padded(jnp.stack([water, south], axis=1), (("space", 2),), 1)


def picker(wanted):

    def fold(carry, pieces, start):
        count = pieces[0].shape[0]
        select = (wanted[:, None] == jnp.arange(count, dtype=jnp.int32)[None, :]).astype(
            jnp.float32
        )
        return tuple(
            (
                jnp.einsum("km,m...->k...", select, piece, precision=lax.Precision.HIGHEST)
                for piece in pieces
            )
        )

    return fold


def shards(depth, flow_x, flow_y, terrain, roughness, gauges, observed, ancestors):
    parts, rows, width = depth.shape
    slab = lax.axis_index("space")
    all_rows = rows * lax.axis_size("space")
    statics = padded(jnp.stack([terrain, roughness]), (("space", 1),), 1)
    depth_rim = 1
    bed_ext = statics[0]
    rough_ext = statics[1]
    bed_own = bed_ext[depth_rim : depth_rim + rows]
    rough_own = rough_ext[depth_rim : depth_rim + rows]
    row_ids = slab * rows - depth_rim + jnp.arange(rows + 2 * depth_rim, dtype=jnp.int32)
    face_ok = ((row_ids[:-1] >= 0) & (row_ids[:-1] < all_rows - 1))[:, None]

    def advance(extended, east_old):
        water_ext = extended[:, 0]
        south_ext = extended[:, 1]
        eta = bed_ext + water_ext
        eta_own = eta[:, 1:-1]
        east = face_flux(
            east_old[:, :, :-1],
            eta_own[:, :, :-1],
            eta_own[:, :, 1:],
            bed_own[:, :-1],
            bed_own[:, 1:],
            rough_own[:, :-1],
        )
        east = jnp.concatenate([east, jnp.zeros((parts, rows, 1), jnp.float32)], axis=2)
        south = face_flux(
            south_ext[:, :-1], eta[:, :-1], eta[:, 1:], bed_ext[:-1], bed_ext[1:], rough_ext[:-1]
        )
        south = jnp.where(face_ok, south, 0.0)
        west = jnp.concatenate([jnp.zeros((parts, rows, 1), jnp.float32), east[:, :, :-1]], axis=2)
        water = water_ext[:, 1:-1] + time_step / cell_size * (
            west - east + south[:, :-1] - south[:, 1:]
        )
        return (water, east, south[:, 1:])

    def expand(water, east, south):
        return (with_rims(water, south), east)

    def run(packed):
        water, east, south = advance(packed[0], packed[1])
        water, east, south = advance(with_rims(water, south), east)
        return (water, east, south)

    water, east, south = run(expand(depth, flow_x, flow_y))
    flat = water.reshape(parts, rows * width)
    offset = gauges - slab * rows * width
    inside = (offset >= 0) & (offset < rows * width)
    values = jnp.take(flat, jnp.clip(offset, 0, rows * width - 1), axis=1)
    misfit = jnp.where(inside[None, :], (values - observed[None, :]) ** 2, 0.0)
    loglik = lax.psum(-0.5 * jnp.sum(misfit, axis=1), "space")
    local_top = jnp.max(loglik)
    top = lax.pmax(local_top, "member")
    total = lax.psum(jnp.sum(jnp.exp(loglik - top)), "member")
    log_weight = loglik - top - jnp.log(total)
    wanted = lax.dynamic_slice_in_dim(ancestors, lax.axis_index("member") * parts, parts)
    fold = picker(wanted)
    empty = jnp.zeros_like(water)
    water, east, south = fold(
        (empty, empty, empty),
        (
            lax.all_gather(water, "member", axis=0, tiled=True),
            lax.all_gather(east, "member", axis=0, tiled=True),
            lax.all_gather(south, "member", axis=0, tiled=True),
        ),
        jnp.int32(0),
    )
    water, east, south = run(expand(water, east, south))
    return (water, east, south, log_weight)


def solution(mesh):
    placed = (
        P("member", "space", None),
        P("member", "space", None),
        P("member", "space", None),
        P("space", None),
        P("space", None),
        P(),
        P(),
        P(),
    )
    return jax.shard_map(
        shards,
        mesh=mesh,
        in_specs=placed,
        out_specs=(
            P("member", "space", None),
            P("member", "space", None),
            P("member", "space", None),
            P("member"),
        ),
        check_vma=False,
    )
```

profile of v0, /device:TPU:120, one launch (start us, length us, event | category | flops | bytes accessed | tf_op | source)
XLA Modules:
  0.0 256.1 jit_solution(407749554174382926)
XLA Ops:
  7.2 1.0 pad_maximum_fusion.18
  8.2 5.7 %collective-permute-start.2 = (f32[2,1,2048]{2,1,0:T(1,128)S(1)}, f32[2,1,2048]{2,1,0:T(1,128)S(1)}, u32[]{:S(2)}, u32[]{:S(2)}) collective-permute-start(f32[2,1,2048]{2,1,0:T(1,128)S(1)} %get-tuple-element.45), channel_id=1, source_target_pairs={{0,1},{1,2},{2,3},{3,4},{4,5},{5,6},{6,7},{7,8},{8,9},{9,10},{10,1... | collective-permute-start | bytes 49160 | tf_op jit(solution)/shard_map/ppermute | solution.py:17
  13.9 1.9 collective-permute-start.3
  15.9 1.1 pad_maximum_fusion.16
  17.0 7.5 %collective-permute-start = (f32[2,2,1,2048]{3,2,0,1:T(1,128)S(1)}, f32[2,2,1,2048]{3,2,0,1:T(1,128)S(1)}, u32[]{:S(2)}, u32[]{:S(2)}) collective-permute-start(f32[2,2,1,2048]{3,2,0,1:T(1,128)S(1)} %get-tuple-element.34), channel_id=1, source_target_pairs={{0,1},{1,2},{2,3},{3,4},{4,5},{5,6},{6,7},{7,8},{8,9},{9,10},{10,1... | collective-permute-start | bytes 98312 | tf_op jit(solution)/shard_map/ppermute | solution.py:17
  24.6 1.9 collective-permute-start.1
  26.5 1.1 multiply_multiply_fusion.1
  27.7 1.0 maximum_maximum_fusion
  28.7 1.0 fusion.22
  29.6 0.9 fusion.23
  30.6 3.4 %collective-permute-done.1 = f32[2,2,1,2048]{3,2,0,1:T(1,128)S(1)} collective-permute-done((f32[2,2,1,2048]{3,2,0,1:T(1,128)S(1)}, f32[2,2,1,2048]{3,2,0,1:T(1,128)S(1)}, u32[]{:S(2)}, u32[]{:S(2)}) %collective-permute-start.1) | collective-permute-done | bytes 32800 | tf_op jit(solution)/shard_map/ppermute | solution.py:20
  34.0 1.1 pad_maximum_fusion
  35.2 0.3 add_divide_fusion.3
  35.6 0.4 divide_select_fusion.3
  36.2 4.2 %collective-permute-start.4 = (f32[2,2,1,2048]{3,2,0,1:T(1,128)S(1)}, f32[2,2,1,2048]{3,2,0,1:T(1,128)S(1)}, u32[]{:S(2)}, u32[]{:S(2)}) collective-permute-start(f32[2,2,1,2048]{3,2,0,1:T(1,128)S(1)} %get-tuple-element.32), channel_id=1, source_target_pairs={{0,1},{1,2},{2,3},{3,4},{4,5},{5,6},{6,7},{7,8},{8,9},{9,10},{10,1... | collective-permute-start | bytes 98312 | tf_op jit(solution)/shard_map/ppermute | solution.py:17
  40.4 3.2 %collective-permute-start.5 = (f32[2,2,1,2048]{3,2,0,1:T(1,128)S(1)}, f32[2,2,1,2048]{3,2,0,1:T(1,128)S(1)}, u32[]{:S(2)}, u32[]{:S(2)}) collective-permute-start(f32[2,2,1,2048]{3,2,0,1:T(1,128)S(1)} %get-tuple-element.33), channel_id=1, source_target_pairs={{1,0},{2,1},{3,2},{4,3},{5,4},{6,5},{7,6},{8,7},{9,8},{10,9},{11,1... | collective-permute-start | bytes 98312 | tf_op jit(solution)/shard_map/ppermute | solution.py:20
  43.6 6.2 %collective-permute-done.5 = f32[2,2,1,2048]{3,2,0,1:T(1,128)S(1)} collective-permute-done((f32[2,2,1,2048]{3,2,0,1:T(1,128)S(1)}, f32[2,2,1,2048]{3,2,0,1:T(1,128)S(1)}, u32[]{:S(2)}, u32[]{:S(2)}) %collective-permute-start.5) | collective-permute-done | bytes 32800 | tf_op jit(solution)/shard_map/ppermute | solution.py:20
  50.0 0.3 add_divide_fusion.2
  50.4 0.4 divide_select_fusion.2
  50.8 1.0 fusion.15
  51.8 0.7 all-gather.4.cloned.1.call-update
  52.6 0.7 all-gather.8.cloned.1.call-update
  53.3 9.4 %copy.45 = f32[2,16,2048]{0,2,1:T(8,128)} copy(f32[2,16,2048]{2,1,0:T(8,128)} %get-tuple-element.38) | data formatting | bytes 524288 | tf_op jit(solution)/shard_map/reshape | solution.py:100
  62.7 6.8 %gather_fusion = f32[512,2]{1,0:T(8,128)S(1)} fusion(f32[2,32768]{0,1:T(8,128)} %bitcast.57, s32[1024]{0:T(1024)S(1)} %pad_clamp_fusion), kind=kCustom, calls=%fused_computation | custom fusion | bytes 10240 | tf_op jit(solution)/shard_map/jit(_take)/gather | solution.py:103
  69.5 0.3 select_reduce_fusion
  69.8 72.5 %psum.14 = f32[2]{0:T(128)S(1)} all-reduce(f32[2]{0:T(128)S(1)} %broadcast_multiply_fusion), channel_id=1, replica_groups=mesh['member'=16,'space'=32] {'space'}, use_global_device_ids=true, to_apply=%region_1.2 | all-reduce | flops 2 | bytes 16 | tf_op jit(solution)/shard_map/psum | solution.py:105
  142.3 0.6 reduce_max.9
  142.9 27.8 %pmax.7 = f32[]{:T(128)} all-reduce(f32[]{:T(128)} %reduce_max.9), channel_id=1, replica_groups=mesh['member'=16,'space'=32] {'member'}, use_global_device_ids=true, to_apply=%region_3.4 | all-reduce | flops 1 | bytes 8 | tf_op jit(solution)/shard_map/pmax | solution.py:107
  170.7 1.2 exponential_reduce_fusion
  172.0 28.3 %psum.15 = f32[]{:T(128)} all-reduce(f32[]{:T(128)} %exponential_reduce_fusion), channel_id=1, replica_groups=mesh['member'=16,'space'=32] {'member'}, use_global_device_ids=true, to_apply=%region_5.6 | all-reduce | flops 1 | bytes 8 | tf_op jit(solution)/shard_map/psum | solution.py:108
  201.1 5.8 %fusion.2 = f32[2,16,2048]{2,0,1:T(2,128)S(1)} fusion(f32[32,16,2048]{2,1,0:T(8,128)} %all-gather.6.cloned.1.call-done, s32[2]{0:T(128)S(1)} %dynamic_slice.3), kind=kOutput, calls=%fused_computation.3 | convolution fusion | flops 25165888 | bytes 4456456 | tf_op jit(solution)/shard_map/km,m...->k.../dot_general | solution.py:46
  206.8 0.2 copy.57
  207.0 5.8 %fusion.4 = f32[2,16,2048]{2,0,1:T(2,128)S(1)} fusion(f32[32,16,2048]{2,1,0:T(8,128)} %all-gather.4.cloned.1.call-done, s32[2]{0:T(128)S(1)} %dynamic_slice.3), kind=kOutput, calls=%fused_computation.5 | convolution fusion | flops 25165888 | bytes 4456456 | tf_op jit(solution)/shard_map/km,m...->k.../dot_general | solution.py:46
  212.8 0.2 copy.58
  213.0 7.8 %collective-permute-start.6 = (f32[2,2,1,2048]{3,2,0,1:T(1,128)S(1)}, f32[2,2,1,2048]{3,2,0,1:T(1,128)S(1)}, u32[]{:S(2)}, u32[]{:S(2)}) collective-permute-start(f32[2,2,1,2048]{3,2,0,1:T(1,128)S(1)} %get-tuple-element.30), channel_id=1, source_target_pairs={{0,1},{1,2},{2,3},{3,4},{4,5},{5,6},{6,7},{7,8},{8,9},{9,10},{10,1... | collective-permute-start | bytes 98312 | tf_op jit(solution)/shard_map/ppermute | solution.py:17
  220.8 2.1 collective-permute-start.7
  223.0 5.8 %fusion = f32[2,16,2047]{2,0,1:T(2,128)S(1)} fusion(f32[32,16,2047]{2,1,0:T(8,128)} %bitcast.62, s32[2]{0:T(128)S(1)} %dynamic_slice.3), kind=kOutput, calls=%fused_computation.1 | convolution fusion | flops 25153600 | bytes 4454280 | tf_op jit(solution)/shard_map/km,m...->k.../dot_general | solution.py:46
  228.8 1.4 collective-permute-done.7
  230.5 0.4 add_divide_fusion.1
  230.9 0.4 divide_select_fusion.1
  231.5 6.1 %collective-permute-start.8 = (f32[2,2,1,2048]{3,2,0,1:T(1,128)S(1)}, f32[2,2,1,2048]{3,2,0,1:T(1,128)S(1)}, u32[]{:S(2)}, u32[]{:S(2)}) collective-permute-start(f32[2,2,1,2048]{3,2,0,1:T(1,128)S(1)} %get-tuple-element.28), channel_id=1, source_target_pairs={{0,1},{1,2},{2,3},{3,4},{4,5},{5,6},{6,7},{7,8},{8,9},{9,10},{10,1... | collective-permute-start | bytes 98312 | tf_op jit(solution)/shard_map/ppermute | solution.py:17
  237.6 1.9 collective-permute-start.9
  239.6 1.1 subtract_subtract_fusion
  240.7 6.4 %collective-permute-done.9 = f32[2,2,1,2048]{3,2,0,1:T(1,128)S(1)} collective-permute-done((f32[2,2,1,2048]{3,2,0,1:T(1,128)S(1)}, f32[2,2,1,2048]{3,2,0,1:T(1,128)S(1)}, u32[]{:S(2)}, u32[]{:S(2)}) %collective-permute-start.9) | collective-permute-done | bytes 32800 | tf_op jit(solution)/shard_map/ppermute | solution.py:20
  247.3 0.3 add_divide_fusion
  247.6 0.4 divide_select_fusion
  248.0 0.7 concatenate.60
  248.7 0.9 fusion.8
  (43 shorter events, 1.5 us)
Async XLA Ops:
  7.2 28.1 %copy-start = (f32[2,16,2048]{2,1,0:T(8,128)S(1)}, f32[2,16,2048]{2,1,0:T(8,128)}, u32[]{:S(2)}) copy-start(f32[2,16,2048]{2,1,0:T(8,128)} %param.9) | copy-start | bytes 786436
  7.2 193.9 %all-gather.6.cloned.1.call-start = ((), (), s32[]{:S(2)}) async-start(), calls=%async_computation.1 | async-start | bytes 4456448 | tf_op jit(solution)/shard_map/all_gather | solution.py:118
  8.2 19.4 %collective-permute-start.2 = (f32[2,1,2048]{2,1,0:T(1,128)S(1)}, f32[2,1,2048]{2,1,0:T(1,128)S(1)}, u32[]{:S(2)}, u32[]{:S(2)}) collective-permute-start(f32[2,1,2048]{2,1,0:T(1,128)S(1)} %get-tuple-element.45), channel_id=1, source_target_pairs={{0,1},{1,2},{2,3},{3,4},{4,5},{5,6},{6,7},{7,8},{8,9},{9,10},{10,1... | collective-permute-start | bytes 49160 | tf_op jit(solution)/shard_map/ppermute | solution.py:17
  13.9 14.7 %collective-permute-start.3 = (f32[2,1,2048]{2,1,0:T(1,128)S(1)}, f32[2,1,2048]{2,1,0:T(1,128)S(1)}, u32[]{:S(2)}, u32[]{:S(2)}) collective-permute-start(f32[2,1,2048]{2,1,0:T(1,128)S(1)} %get-tuple-element.46), channel_id=1, source_target_pairs={{1,0},{2,1},{3,2},{4,3},{5,4},{6,5},{7,6},{8,7},{9,8},{10,9},{11,1... | collective-permute-start | bytes 49160 | tf_op jit(solution)/shard_map/ppermute | solution.py:20
  17.0 13.6 %collective-permute-start = (f32[2,2,1,2048]{3,2,0,1:T(1,128)S(1)}, f32[2,2,1,2048]{3,2,0,1:T(1,128)S(1)}, u32[]{:S(2)}, u32[]{:S(2)}) collective-permute-start(f32[2,2,1,2048]{3,2,0,1:T(1,128)S(1)} %get-tuple-element.34), channel_id=1, source_target_pairs={{0,1},{1,2},{2,3},{3,4},{4,5},{5,6},{6,7},{7,8},{8,9},{9,10},{10,1... | collective-permute-start | bytes 98312 | tf_op jit(solution)/shard_map/ppermute | solution.py:17
  24.6 9.4 %collective-permute-start.1 = (f32[2,2,1,2048]{3,2,0,1:T(1,128)S(1)}, f32[2,2,1,2048]{3,2,0,1:T(1,128)S(1)}, u32[]{:S(2)}, u32[]{:S(2)}) collective-permute-start(f32[2,2,1,2048]{3,2,0,1:T(1,128)S(1)} %get-tuple-element.35), channel_id=1, source_target_pairs={{1,0},{2,1},{3,2},{4,3},{5,4},{6,5},{7,6},{8,7},{9,8},{10,9},{11,1... | collective-permute-start | bytes 98312 | tf_op jit(solution)/shard_map/ppermute | solution.py:20
  36.2 7.4 %collective-permute-start.4 = (f32[2,2,1,2048]{3,2,0,1:T(1,128)S(1)}, f32[2,2,1,2048]{3,2,0,1:T(1,128)S(1)}, u32[]{:S(2)}, u32[]{:S(2)}) collective-permute-start(f32[2,2,1,2048]{3,2,0,1:T(1,128)S(1)} %get-tuple-element.32), channel_id=1, source_target_pairs={{0,1},{1,2},{2,3},{3,4},{4,5},{5,6},{6,7},{7,8},{8,9},{9,10},{10,1... | collective-permute-start | bytes 98312 | tf_op jit(solution)/shard_map/ppermute | solution.py:17
  40.4 9.4 %collective-permute-start.5 = (f32[2,2,1,2048]{3,2,0,1:T(1,128)S(1)}, f32[2,2,1,2048]{3,2,0,1:T(1,128)S(1)}, u32[]{:S(2)}, u32[]{:S(2)}) collective-permute-start(f32[2,2,1,2048]{3,2,0,1:T(1,128)S(1)} %get-tuple-element.33), channel_id=1, source_target_pairs={{1,0},{2,1},{3,2},{4,3},{5,4},{6,5},{7,6},{8,7},{9,8},{10,9},{11,1... | collective-permute-start | bytes 98312 | tf_op jit(solution)/shard_map/ppermute | solution.py:20
  49.9 3.4 %copy-start.2 = (s32[512]{0:T(512)S(1)}, s32[512]{0:T(512)}, u32[]{:S(2)}) copy-start(s32[512]{0:T(512)} %param.13) | copy-start | bytes 6148
  51.8 155.2 %all-gather.4.cloned.1.call-start = ((), (), s32[]{:S(2)}) async-start(), calls=%async_computation | async-start | bytes 4456448 | tf_op jit(solution)/shard_map/all_gather | solution.py:116
  52.5 170.5 %all-gather.8.cloned.1.call-start = ((), (), s32[]{:S(2)}) async-start(), calls=%async_computation.2 | async-start | bytes 4456448 | tf_op jit(solution)/shard_map/all_gather | solution.py:117
  53.3 16.2 %copy-start.1 = (f32[512]{0:T(512)S(1)}, f32[512]{0:T(512)}, u32[]{:S(2)}) copy-start(f32[512]{0:T(512)} %param.14) | copy-start | bytes 6148
  53.3 118.6 %copy-start.3 = (s32[32]{0:T(128)S(1)}, s32[32]{0:T(128)}, u32[]{:S(2)}) copy-start(s32[32]{0:T(128)} %param.15) | copy-start | bytes 388
  213.0 15.8 %collective-permute-start.6 = (f32[2,2,1,2048]{3,2,0,1:T(1,128)S(1)}, f32[2,2,1,2048]{3,2,0,1:T(1,128)S(1)}, u32[]{:S(2)}, u32[]{:S(2)}) collective-permute-start(f32[2,2,1,2048]{3,2,0,1:T(1,128)S(1)} %get-tuple-element.30), channel_id=1, source_target_pairs={{0,1},{1,2},{2,3},{3,4},{4,5},{5,6},{6,7},{7,8},{8,9},{9,10},{10,1... | collective-permute-start | bytes 98312 | tf_op jit(solution)/shard_map/ppermute | solution.py:17
  220.8 9.4 %collective-permute-start.7 = (f32[2,2,1,2048]{3,2,0,1:T(1,128)S(1)}, f32[2,2,1,2048]{3,2,0,1:T(1,128)S(1)}, u32[]{:S(2)}, u32[]{:S(2)}) collective-permute-start(f32[2,2,1,2048]{3,2,0,1:T(1,128)S(1)} %get-tuple-element.31), channel_id=1, source_target_pairs={{1,0},{2,1},{3,2},{4,3},{5,4},{6,5},{7,6},{8,7},{9,8},{10,9},{11,1... | collective-permute-start | bytes 98312 | tf_op jit(solution)/shard_map/ppermute | solution.py:20
  231.5 9.2 %collective-permute-start.8 = (f32[2,2,1,2048]{3,2,0,1:T(1,128)S(1)}, f32[2,2,1,2048]{3,2,0,1:T(1,128)S(1)}, u32[]{:S(2)}, u32[]{:S(2)}) collective-permute-start(f32[2,2,1,2048]{3,2,0,1:T(1,128)S(1)} %get-tuple-element.28), channel_id=1, source_target_pairs={{0,1},{1,2},{2,3},{3,4},{4,5},{5,6},{6,7},{7,8},{8,9},{9,10},{10,1... | collective-permute-start | bytes 98312 | tf_op jit(solution)/shard_map/ppermute | solution.py:17
  237.6 9.4 %collective-permute-start.9 = (f32[2,2,1,2048]{3,2,0,1:T(1,128)S(1)}, f32[2,2,1,2048]{3,2,0,1:T(1,128)S(1)}, u32[]{:S(2)}, u32[]{:S(2)}) collective-permute-start(f32[2,2,1,2048]{3,2,0,1:T(1,128)S(1)} %get-tuple-element.29), channel_id=1, source_target_pairs={{1,0},{2,1},{3,2},{4,3},{5,4},{6,5},{7,6},{8,7},{9,8},{10,9},{11,1... | collective-permute-start | bytes 98312 | tf_op jit(solution)/shard_map/ppermute | solution.py:20
Sparse Core Ops, SparseCore 0:
  51.9 45.0 all-gather.5
  99.7 45.3 all-gather.3
  147.8 45.2 all-gather.7
where the time goes:
time: 258 us; the launch traced here: 256 us
  blocking collectives  129 us (50%)
  starting transfers between devices  42.5 us (16%)
  waiting for transfers between devices  18.9 us (7%)
  local copies, waits for them, and re-layouts  17.5 us (7%)
  matrix products  17.4 us (7%)
  other arithmetic  16.4 us (6%)
  between operations  14.9 us (6%)
    psum x1, blocking collectives, shards(): loglik = lax.psum(-0.5 * jnp.sum(misfit, axis=1), 'space')  72.5 us
    ppermute x5, starting transfers between devices, padded(): lax.ppermute(lax.slice_in_dim(block, block.shape[dim] - width, None, axis...  31.3 us
    psum x1, blocking collectives, shards(): total = lax.psum(jnp.sum(jnp.exp(loglik - top)), 'member')  28.3 us
    pmax x1, blocking collectives, shards(): top = lax.pmax(local_top, 'member')  27.8 us
    ppermute x5, waiting for transfers between devices, padded(): lax.ppermute(lax.slice_in_dim(block, 0, width, axis=dim), axis, backward)  17.4 us
    dot_general x3, matrix products, fold(): jnp.einsum('km,m...->k...', select, piece, precision=lax.Precision.HIGHEST)  17.4 us
    ppermute x5, starting transfers between devices, padded(): lax.ppermute(lax.slice_in_dim(block, 0, width, axis=dim), axis, backward)  11.1 us
    reshape x1, local copies, waits for them, and re-layouts, shards(): flat = water.reshape(parts, rows * width)  9.36 us
  transfers between devices with their start and end apart: 13, of which 4 were waited for; matrix products, arithmetic and copies ran while one was open for 17% of the time, Pallas kernels for 0%

commit v1 on v0

v1 whole, which is shorter than its diff:
```python
import functools

import jax
import jax.numpy as jnp
from jax import lax
from jax.experimental import pallas as pl
from jax.experimental.pallas import tpu as pltpu
from jax.sharding import PartitionSpec as P

MESH = pl.DeviceIdType.MESH
gravity = 9.81
time_step = 1.0
cell_size = 30.0
depth_floor = 0.1

EAST, WATER, SOUTH = 0, 1, 2
ROWS = 16
LANES = 128
PARTS = 2
SUB = 16
RIM = 2
EXT = ROWS + 2 * RIM
BARS = (4, 4, 2)
HOLDERS = 9
VMEM_LIMIT = 48 * 2**20


def next_column(x):
    y = pltpu.roll(x, LANES - 1, 1)
    lane = lax.broadcasted_iota(jnp.int32, x.shape, 1)
    return jnp.where(lane == LANES - 1, pltpu.roll(y, SUB - 1, 0), y)


def previous_column(x):
    y = pltpu.roll(x, 1, 1)
    lane = lax.broadcasted_iota(jnp.int32, x.shape, 1)
    return jnp.where(lane == 0, pltpu.roll(y, 1, 0), y)


def face(flow, eta_a, eta_b, bed_top, friction):
    hflow = jnp.maximum(jnp.maximum(eta_a, eta_b) - bed_top, depth_floor)
    push = flow - (gravity * time_step / cell_size) * hflow * (eta_b - eta_a)
    drag = 1.0 + friction * jnp.abs(flow) * jnp.exp(jnp.log(hflow) * (-7.0 / 3.0))
    inverse = pl.reciprocal(drag, approx=True)
    inverse = inverse * (2.0 - drag * inverse)
    return push * inverse


def south_flow(src, bed, row, first, last_row):
    at = row + RIM
    bed_a, bed_b = bed[at, 0], bed[at + 1, 0]
    bed_top = jnp.maximum(bed_a, bed_b)
    friction = bed[at, 1]
    ok = jnp.logical_and(first + row >= 0, first + row < last_row)
    out = []
    for p in range(PARTS):
        eta_a = bed_a + src[3 * at + WATER, p]
        eta_b = bed_b + src[3 * (at + 1) + WATER, p]
        flow = face(src[3 * at + SOUTH, p], eta_a, eta_b, bed_top, friction)
        out.append(jnp.where(ok, flow, 0.0))
    return tuple(out)


def step_rows(src, bed, low, count, first, last_row, store):
    sub = lax.broadcasted_iota(jnp.int32, (SUB, LANES), 0)
    lane = lax.broadcasted_iota(jnp.int32, (SUB, LANES), 1)
    rim = jnp.logical_and(sub == SUB - 1, lane == LANES - 1)

    def one(i, north):
        row = low + i
        at = row + RIM
        south = south_flow(src, bed, row, first, last_row)
        bed_a = bed[at, 0]
        bed_top = jnp.maximum(bed_a, next_column(bed_a))
        friction = bed[at, 1]
        for p in range(PARTS):
            water = src[3 * at + WATER, p]
            eta = bed_a + water
            east = face(src[3 * at + EAST, p], eta, next_column(eta), bed_top, friction)
            east = jnp.where(rim, 0.0, east)
            west = previous_column(east)
            new = water + (time_step / cell_size) * (west - east + north[p] - south[p])
            store(row, p, EAST, east)
            store(row, p, WATER, new)
            store(row, p, SOUTH, south[p])
        return south

    lax.fori_loop(0, count, one, south_flow(src, bed, low - 1, first, last_row))


def keep_in(dst, rim):
    def store(row, p, field, value):
        dst[3 * (row + rim) + field, p] = value

    return store


def exchange_kernel(
    members, slabs,
    water_in, east_in, south_in, bed_in, rough_in, gauges, observed, ancestors,
    state_out, bed_out, lik_out,
    raw, raw_bed, a, b, c, bed, held, held_rim, out, out_rim, sums, got,
    in_sem, halo_send, halo_recv, s1, r1, sh, rh, s2, r2, s2h, r2h, ls, lr, ms, mr, own_sem,
):
    m = lax.axis_index("member")
    s = lax.axis_index("space")
    up = lax.rem(s + slabs - 1, slabs)
    down = lax.rem(s + 1, slabs)
    across = lax.rem(m + members // 2, members)
    first = s * ROWS
    last_row = slabs * ROWS - 1
    rim_at = m // 2 + 8 * lax.rem(m, 2)
    rim_slot = 1 + rim_at + 48 * (rim_at // 5) + rim_at // 8

    def remote(src, dst, send, recv, member, slab):
        return pltpu.make_async_remote_copy(
            src_ref=src, dst_ref=dst, send_sem=send, recv_sem=recv,
            device_id=(member, slab), device_id_type=MESH,
        )

    loads = [
        pltpu.make_async_copy(ref, raw.at[i], in_sem.at[i])
        for i, ref in enumerate((east_in, water_in, south_in))
    ] + [
        pltpu.make_async_copy(ref, raw_bed.at[i], in_sem.at[3 + i])
        for i, ref in enumerate((bed_in, rough_in))
    ]
    for copy in loads:
        copy.start()

    ring = []
    stride = 1
    for size in BARS:
        digit = lax.rem(s // stride, size)
        ring.append([
            s + (lax.rem(digit + i, size) - digit) * stride for i in range(1, size)
        ])
        stride *= size
    holder = [(2 * i if i < 8 else 1, down if i < 5 else up) for i in range(HOLDERS)]

    barrier = pltpu.get_barrier_semaphore()

    def greet(member, slab):
        pl.semaphore_signal(barrier, inc=1, device_id=(member, slab), device_id_type=MESH)

    for slab in (up, down):
        greet(m, slab)
        greet(across, slab)

    @pl.loop(1, members)
    def _(i):
        greet(lax.rem(m + i, members), s)

    @pl.when(rim_at < 5)
    def _():
        @pl.loop(0, members)
        def _(i):
            greet(i, up)

    @pl.when(jnp.logical_and(rim_at >= 5, rim_at < HOLDERS))
    def _():
        @pl.loop(0, members)
        def _(i):
            greet(i, down)

    for partners in ring:
        for slab in partners:
            greet(m, slab)

    for copy in loads:
        copy.wait()

    @pl.loop(0, ROWS)
    def _(r):
        from_row = (r // 8) * (8 * SUB) + lax.rem(r, 8)
        for i in range(3):
            for p in range(PARTS):
                a[3 * (r + RIM) + i, p] = raw[i, pl.ds(p * ROWS * SUB + from_row, SUB, stride=8)]
        bed[r + RIM, 0] = raw_bed[0, pl.ds(from_row, SUB, stride=8)]
        rough = raw_bed[1, pl.ds(from_row, SUB, stride=8)]
        bed[r + RIM, 1] = (gravity * time_step) * rough * rough

    step_rows(a, bed, 1, ROWS - 2, first, last_row, keep_in(b, RIM))
    step_rows(b, bed, 2, ROWS - 4, first, last_row, keep_in(c, 0))

    pl.semaphore_wait(barrier, members - 1 + 4 + sum(n - 1 for n in BARS) + HOLDERS)

    low, high = 3 * RIM, 3 * (RIM + ROWS)
    halos = [
        remote(bed.at[pl.ds(ROWS, RIM)], bed.at[pl.ds(0, RIM)], halo_send.at[0], halo_recv.at[0], across, down),
        remote(bed.at[pl.ds(RIM, RIM)], bed.at[pl.ds(RIM + ROWS, RIM)], halo_send.at[1], halo_recv.at[1], across, up),
        remote(a.at[pl.ds(high - 5, 5)], a.at[pl.ds(low - 5, 5)], halo_send.at[2], halo_recv.at[2], m, down),
        remote(a.at[pl.ds(low, 3)], a.at[pl.ds(high, 3)], halo_send.at[3], halo_recv.at[3], m, up),
        remote(a.at[pl.ds(low + 4, 1)], a.at[pl.ds(high + 4, 1)], halo_send.at[4], halo_recv.at[4], m, up),
    ]
    for copy in halos:
        copy.start()

    def spread(to):
        return remote(c.at[pl.ds(3 * to, 3)], held.at[m], s1.at[to], r1.at[m], to, s)

    def spread_from(source):
        return remote(c.at[pl.ds(0, 3)], held.at[source], s1.at[source], r1.at[source], source, s)

    def inner(j):
        return jnp.logical_and(j >= 2, j < ROWS - 2)

    @pl.loop(1, members)
    def _(i):
        to = lax.rem(m + i, members)

        @pl.when(inner(to))
        def _():
            spread(to).start()

    for copy in halos:
        copy.wait_recv()

    step_rows(a, bed, -1, 2, first, last_row, keep_in(b, RIM))
    step_rows(a, bed, ROWS - 1, 2, first, last_row, keep_in(b, RIM))
    step_rows(b, bed, 0, 2, first, last_row, keep_in(c, 0))
    step_rows(b, bed, ROWS - 2, 2, first, last_row, keep_in(c, 0))

    rim_slots = [3 * ROWS - 5 + i for i in range(5)] + [0, 1, 2, 4]
    rims = [
        remote(c.at[rim_slots[i]], held_rim.at[m], sh.at[i], rh.at[m], member, slab)
        for i, (member, slab) in enumerate(holder)
    ]
    for copy in rims:
        copy.start()

    @pl.loop(1, members)
    def _(i):
        to = lax.rem(m + i, members)

        @pl.when(jnp.logical_not(inner(to)))
        def _():
            spread(to).start()

    held[m] = c[pl.ds(3 * m, 3)]
    bed_copy = pltpu.make_async_copy(bed, bed_out, own_sem.at[0])
    bed_copy.start()

    cell = gauges[...] - first * (SUB * LANES)
    block = cell >> 7
    lane = cell & (LANES - 1)
    count = cell.shape[1]
    blocks = ROWS * SUB
    pick = jnp.where(
        lax.broadcasted_iota(jnp.int32, (blocks, count), 0) == block, 1.0, 0.0
    ).astype(jnp.bfloat16)
    inside = jnp.logical_and(block >= 0, block < blocks)
    here = jnp.logical_and(
        lax.broadcasted_iota(jnp.int32, (LANES, count), 0) == lane, inside
    )
    totals = []
    for p in range(PARTS):
        water = jnp.concatenate([c[3 * r + WATER, p] for r in range(ROWS)], axis=0).T
        value = jnp.zeros((LANES, count), jnp.float32)
        for _ in range(3):
            part = water.astype(jnp.bfloat16)
            value += jnp.dot(part, pick, preferred_element_type=jnp.float32)
            water = water - part.astype(jnp.float32)
        misfit = jnp.where(here, (value - observed[...]) ** 2, 0.0)
        total = jnp.sum(misfit, axis=0, keepdims=True)
        totals.append(sum(total[:, i : i + LANES] for i in range(0, count, LANES)))
    sub = lax.broadcasted_iota(jnp.int32, (8, LANES), 0)
    sums[0] = jnp.where(sub == 0, totals[0], jnp.where(sub == 1, totals[1], 0.0))

    def stage(t):
        base = sum(n - 1 for n in BARS[:t])
        return [
            remote(sums.at[t], got.at[base + i], ls.at[base + i], lr.at[base + i], m, slab)
            for i, slab in enumerate(ring[t])
        ]

    def fold(t, copies):
        base = sum(n - 1 for n in BARS[:t])
        value = sums[t]
        for i, copy in enumerate(copies):
            copy.wait_recv()
            value = value + got[base + i]
        sums[t + 1] = value

    stages = [stage(0)]
    for copy in stages[0]:
        copy.start()

    @pl.loop(1, members)
    def _(i):
        spread_from(lax.rem(m + i, members)).wait_recv()

    @pl.when(rim_at < HOLDERS)
    def _():
        @pl.loop(0, members)
        def _(i):
            remote(c.at[0], held_rim.at[i], sh.at[0], rh.at[i], i, down).wait_recv()

    def route(to):
        return remote(out.at[to], state_out.at[pl.ds(3 * (m + RIM), 3)], s2.at[to], r2.at[m], to, s)

    def route_from(source):
        return remote(out.at[source], state_out.at[pl.ds(3 * (source + RIM), 3)], s2.at[source], r2.at[source], source, s)

    def route_rim(to):
        return remote(out_rim.at[to], state_out.at[rim_slot], s2h.at[to], r2h.at[rim_at], to, s)

    def wanted(to):
        for k in range(PARTS):
            q = ancestors[PARTS * to + k]
            for f in range(3):
                out[to, f, k] = held[q // PARTS, f, lax.rem(q, PARTS)]

    def wanted_rim(to):
        for k in range(PARTS):
            q = ancestors[PARTS * to + k]
            out_rim[to, k] = held_rim[q // PARTS, lax.rem(q, PARTS)]

    @pl.loop(1, members)
    def _(i):
        to = lax.rem(m + i, members)
        wanted(to)
        route(to).start()

        @pl.when(rim_at < HOLDERS)
        def _():
            wanted_rim(to)
            route_rim(to).start()

    wanted(m)
    mine = pltpu.make_async_copy(out.at[m], state_out.at[pl.ds(3 * (m + RIM), 3)], own_sem.at[1])
    mine.start()

    @pl.when(rim_at < HOLDERS)
    def _():
        wanted_rim(m)
        pltpu.make_async_copy(out_rim.at[m], state_out.at[rim_slot], own_sem.at[2]).start()

    for t in range(len(BARS)):
        fold(t, stages[t])
        if t + 1 < len(BARS):
            stages.append(stage(t + 1))
            for copy in stages[t + 1]:
                copy.start()

    final = sums.at[len(BARS)]

    def tell(to):
        return remote(final, lik_out.at[m], ms.at[to], mr.at[m], to, s)

    @pl.loop(1, members)
    def _(i):
        tell(lax.rem(m + i, members)).start()

    mine_lik = pltpu.make_async_copy(final, lik_out.at[m], own_sem.at[3])
    mine_lik.start()

    for copy in halos + rims:
        copy.wait_send()
    for copies in stages:
        for copy in copies:
            copy.wait_send()

    @pl.loop(1, members)
    def _(i):
        to = lax.rem(m + i, members)
        spread(to).wait_send()
        route(to).wait_send()
        tell(to).wait_send()

        @pl.when(rim_at < HOLDERS)
        def _():
            route_rim(to).wait_send()

    @pl.loop(1, members)
    def _(i):
        source = lax.rem(m + i, members)
        route_from(source).wait_recv()
        remote(final, lik_out.at[source], ms.at[source], mr.at[source], source, s).wait_recv()

    for i, (member, _) in enumerate(holder):
        slot = 1 + i + 48 * (i // 5) + i // 8

        @pl.when(m != member)
        def _(i=i, slot=slot, member=member):
            remote(out_rim.at[0], state_out.at[slot], s2h.at[0], r2h.at[i], member, s).wait_recv()

    bed_copy.wait()
    mine.wait()
    mine_lik.wait()

    @pl.when(rim_at < HOLDERS)
    def _():
        pltpu.make_async_copy(out_rim.at[m], state_out.at[rim_slot], own_sem.at[2]).wait()


def finish_kernel(
    slabs, state_in, bed_in, lik_in, water_out, east_out, south_out, weight_out,
    a, b, bed, lik, done, in_sem, out_sem,
):
    m = lax.axis_index("member")
    s = lax.axis_index("space")
    first = s * ROWS
    last_row = slabs * ROWS - 1
    loads = [
        pltpu.make_async_copy(src, dst, in_sem.at[i])
        for i, (src, dst) in enumerate(((state_in, a), (bed_in, bed), (lik_in, lik)))
    ]
    for copy in loads:
        copy.start()
    for copy in loads:
        copy.wait()
    step_rows(a, bed, -1, EXT - 2, first, last_row, keep_in(b, RIM))

    def store(row, p, field, value):
        start = p * ROWS * SUB + (row // 8) * (8 * SUB) + lax.rem(row, 8)
        done[field, pl.ds(start, SUB, stride=8)] = value

    step_rows(b, bed, 0, ROWS, first, last_row, store)
    copies = [
        pltpu.make_async_copy(done.at[i], ref, out_sem.at[i])
        for i, ref in enumerate((east_out, water_out, south_out))
    ]
    for copy in copies:
        copy.start()

    total = -0.5 * jnp.sum(lik[...], axis=2, keepdims=True)
    total = jnp.broadcast_to(total, lik.shape)
    named = lax.broadcasted_iota(jnp.int32, lik.shape, 1) < PARTS
    top = jnp.max(jnp.where(named, total, -jnp.inf), axis=(0, 1), keepdims=True)
    shifted = total - top
    mass = jnp.sum(jnp.where(named, jnp.exp(jnp.where(named, shifted, 0.0)), 0.0), axis=(0, 1), keepdims=True)
    lik[...] = shifted - jnp.log(mass)
    own = lik[m]
    sub = lax.broadcasted_iota(jnp.int32, own.shape, 0)
    lane = lax.broadcasted_iota(jnp.int32, own.shape, 1)
    for p in range(PARTS):
        weight_out[p] = jnp.sum(jnp.where(jnp.logical_and(sub == p, lane == 0), own, 0.0))
    for copy in copies:
        copy.wait()


def to_blocks(x):
    lead = x.shape[:-2]
    n = len(lead)
    x = x.reshape(*lead, x.shape[-2] // 8, 8, SUB, LANES)
    x = x.transpose(*range(n), n, n + 2, n + 1, n + 3)
    return x.reshape(-1, LANES)


def from_blocks(x, parts, rows, width):
    x = x.reshape(parts, rows // 8, SUB, 8, LANES).transpose(0, 1, 3, 2, 4)
    return x.reshape(parts, rows, width)


def shards(members, slabs, depth, flow_x, flow_y, terrain, roughness, gauges, observed, ancestors):
    parts, rows, width = depth.shape
    f32 = jnp.float32
    hbm = pl.BlockSpec(memory_space=pl.ANY)
    vmem = pl.BlockSpec(memory_space=pltpu.VMEM)
    smem = pl.BlockSpec(memory_space=pltpu.SMEM)
    row = (PARTS, SUB, LANES)
    dma = pltpu.SemaphoreType.DMA
    stages = sum(n - 1 for n in BARS)
    cells = parts * rows * SUB
    state, bed, lik = pl.pallas_call(
        functools.partial(exchange_kernel, members, slabs),
        out_shape=(
            jax.ShapeDtypeStruct((3 * EXT, *row), f32),
            jax.ShapeDtypeStruct((EXT, 2, SUB, LANES), f32),
            jax.ShapeDtypeStruct((members, 8, LANES), f32),
        ),
        in_specs=[hbm] * 5 + [vmem] * 2 + [smem],
        out_specs=(hbm, hbm, hbm),
        scratch_shapes=[
            pltpu.VMEM((3, cells, LANES), f32),
            pltpu.VMEM((2, rows * SUB, LANES), f32),
            pltpu.VMEM((3 * EXT, *row), f32),
            pltpu.VMEM((3 * EXT, *row), f32),
            pltpu.VMEM((3 * ROWS, *row), f32),
            pltpu.VMEM((EXT, 2, SUB, LANES), f32),
            pltpu.VMEM((members, 3, *row), f32),
            pltpu.VMEM((members, *row), f32),
            pltpu.VMEM((members, 3, *row), f32),
            pltpu.VMEM((members, *row), f32),
            pltpu.VMEM((len(BARS) + 1, 8, LANES), f32),
            pltpu.VMEM((stages, 8, LANES), f32),
            dma((5,)),
            dma((5,)), dma((5,)),
            dma((members,)), dma((members,)),
            dma((HOLDERS,)), dma((members,)),
            dma((members,)), dma((members,)),
            dma((members,)), dma((HOLDERS,)),
            dma((stages,)), dma((stages,)),
            dma((members,)), dma((members,)),
            dma((4,)),
        ],
        compiler_params=pltpu.CompilerParams(
            collective_id=0, has_side_effects=True, vmem_limit_bytes=VMEM_LIMIT
        ),
        name="exchange",
    )(
        to_blocks(depth), to_blocks(flow_x), to_blocks(flow_y), to_blocks(terrain), to_blocks(roughness),
        gauges.reshape(1, -1), observed.reshape(1, -1), ancestors,
    )
    water, east, south, weight = pl.pallas_call(
        functools.partial(finish_kernel, slabs),
        out_shape=(jax.ShapeDtypeStruct((cells, LANES), f32),) * 3
        + (jax.ShapeDtypeStruct((parts,), f32),),
        in_specs=[hbm] * 3,
        out_specs=(hbm, hbm, hbm, smem),
        scratch_shapes=[
            pltpu.VMEM((3 * EXT, *row), f32),
            pltpu.VMEM((3 * EXT, *row), f32),
            pltpu.VMEM((EXT, 2, SUB, LANES), f32),
            pltpu.VMEM((members, 8, LANES), f32),
            pltpu.VMEM((3, cells, LANES), f32),
            dma((3,)), dma((3,)),
        ],
        compiler_params=pltpu.CompilerParams(vmem_limit_bytes=VMEM_LIMIT),
        name="finish",
    )(state, bed, lik)
    back = functools.partial(from_blocks, parts=parts, rows=rows, width=width)
    return back(water), back(east), back(south), weight


def solution(mesh):
    placed = (P("member", "space", None),) * 3 + (P("space", None),) * 2 + (P(),) * 3
    return jax.shard_map(
        functools.partial(shards, mesh.shape["member"], mesh.shape["space"]),
        mesh=mesh,
        in_specs=placed,
        out_specs=(P("member", "space", None),) * 3 + (P("member"),),
        check_vma=False,
    )
```

time: 258 us -> 74.3 us (0.29)
  the two profiles are of different devices: /device:TPU:120 before, /device:TPU:1 now
where the time goes in v1:
time: 74.3 us; the launch traced here: 74 us
  Pallas kernels  68 us (92%)
  local copies, waits for them, and re-layouts  5.33 us (7%)
    pallas_call x1, Pallas kernels, shards(): pl.pallas_call(functools.partial(exchange_kernel, members, slabs), out_sh...  59.8 us
    pallas_call x1, Pallas kernels, shards(): pl.pallas_call(functools.partial(finish_kernel, slabs), out_shape=(jax.Sh...  8.25 us
    unnamed x16, local copies, waits for them, and re-layouts  5.33 us

profile of v1, /device:TPU:1, one launch (start us, length us, event | category | flops | bytes accessed | tf_op | source)
XLA Modules:
  0.0 74.0 jit_solution(8781035009834986944)
XLA Ops:
  0.6 0.0 copy-start.6
  0.6 0.0 copy-start.5
  0.7 0.0 copy-start.7
  0.7 0.7 copy-done.6
  1.3 0.0 copy-done.5
  1.3 0.0 copy-done.7
  1.3 0.0 copy-start
  1.3 0.9 %copy-done = f32[2,16,2048]{2,1,0:T(8,128)S(1)} copy-done((f32[2,16,2048]{2,1,0:T(8,128)S(1)}, f32[2,16,2048]{2,1,0:T(8,128)}, u32[]{:S(2)}) %copy-start) | copy-done | bytes 262168
  2.3 0.0 copy-start.1
  2.3 0.9 %copy-done.1 = f32[2,16,2048]{2,1,0:T(8,128)S(1)} copy-done((f32[2,16,2048]{2,1,0:T(8,128)S(1)}, f32[2,16,2048]{2,1,0:T(8,128)}, u32[]{:S(2)}) %copy-start.1) | copy-done | bytes 262168
  3.2 0.0 copy-start.2
  3.2 0.9 %copy-done.2 = f32[2,16,2048]{2,1,0:T(8,128)S(1)} copy-done((f32[2,16,2048]{2,1,0:T(8,128)S(1)}, f32[2,16,2048]{2,1,0:T(8,128)}, u32[]{:S(2)}) %copy-start.2) | copy-done | bytes 262168
  4.2 0.0 copy-start.3
  4.2 0.9 %copy-done.3 = f32[16,2048]{1,0:T(8,128)S(1)} copy-done((f32[16,2048]{1,0:T(8,128)S(1)}, f32[16,2048]{1,0:T(8,128)}, u32[]{:S(2)}) %copy-start.3) | copy-done | bytes 131096
  5.1 0.0 copy-start.4
  5.1 0.9 %copy-done.4 = f32[16,2048]{1,0:T(8,128)S(1)} copy-done((f32[16,2048]{1,0:T(8,128)S(1)}, f32[16,2048]{1,0:T(8,128)}, u32[]{:S(2)}) %copy-start.4) | copy-done | bytes 131096
  6.0 59.8 %exchange.1 = (f32[60,2,16,128]{3,2,1,0:T(8,128)S(1)}, f32[20,2,16,128]{3,2,1,0:T(8,128)S(1)}, f32[16,8,128]{2,1,0:T(8,128)S(1)}) custom-call(f32[512,128]{1,0:T(8,128)S(1)} %bitcast.42, f32[512,128]{1,0:T(8,128)S(1)} %bitcast.43, f32[512,128]{1,0:T(8,128)S(1)} %bitcast.44, f32[256,128]{1,0:T(8,128)S(1)} %bitcast.45, f32[256,128]{1,0:T(8,128)S(1)} %bitcast.46, ...), custom_call_target="tpu_custom_call" | custom-call | tf_op jit(solution)/shard_map/exchange/pallas_call | solution.py:466
  65.8 8.2 %finish.1 = (f32[512,128]{1,0:T(8,128)}, f32[512,128]{1,0:T(8,128)}, f32[512,128]{1,0:T(8,128)}, f32[2]{0:T(128)}) custom-call(f32[60,2,16,128]{3,2,1,0:T(8,128)S(1)} %get-tuple-element.11.state_in, f32[20,2,16,128]{3,2,1,0:T(8,128)S(1)} %get-tuple-element.12.bed_in, f32[16,8,128]{2,1,0:T(8,128)S(1)} %get-tuple-element.13.lik_in), custom_call_target="tpu_custom_call" | custom-call | tf_op jit(solution)/shard_map/finish/pallas_call | solution.py:506
Async XLA Ops:
  0.6 0.7 copy-start.6
  0.6 0.7 copy-start.5
  0.7 0.7 copy-start.7
  1.3 1.0 %copy-start = (f32[2,16,2048]{2,1,0:T(8,128)S(1)}, f32[2,16,2048]{2,1,0:T(8,128)}, u32[]{:S(2)}) copy-start(f32[2,16,2048]{2,1,0:T(8,128)} %param.8) | copy-start | bytes 786436
  2.3 0.9 %copy-start.1 = (f32[2,16,2048]{2,1,0:T(8,128)S(1)}, f32[2,16,2048]{2,1,0:T(8,128)}, u32[]{:S(2)}) copy-start(f32[2,16,2048]{2,1,0:T(8,128)} %param.9) | copy-start | bytes 786436
  3.2 0.9 %copy-start.2 = (f32[2,16,2048]{2,1,0:T(8,128)S(1)}, f32[2,16,2048]{2,1,0:T(8,128)}, u32[]{:S(2)}) copy-start(f32[2,16,2048]{2,1,0:T(8,128)} %param.10) | copy-start | bytes 786436
  4.2 0.9 %copy-start.3 = (f32[16,2048]{1,0:T(8,128)S(1)}, f32[16,2048]{1,0:T(8,128)}, u32[]{:S(2)}) copy-start(f32[16,2048]{1,0:T(8,128)} %param.11) | copy-start | bytes 393220
  5.1 0.9 %copy-start.4 = (f32[16,2048]{1,0:T(8,128)S(1)}, f32[16,2048]{1,0:T(8,128)}, u32[]{:S(2)}) copy-start(f32[16,2048]{1,0:T(8,128)} %param.12) | copy-start | bytes 393220

commit v2 on v1

v2 whole, which is shorter than its diff:
```python
import functools

import jax
import jax.numpy as jnp
from jax import lax
from jax.experimental import pallas as pl
from jax.experimental.pallas import tpu as pltpu
from jax.sharding import PartitionSpec as P

MESH = pl.DeviceIdType.MESH
gravity = 9.81
time_step = 1.0
cell_size = 30.0
depth_floor = 0.1

EAST, WATER, SOUTH = 0, 1, 2
ROWS = 16
LANES = 128
PARTS = 2
SUB = 16
RIM = 2
EXT = ROWS + 2 * RIM
HOLDERS = 9
VMEM_LIMIT = 60 * 2**20


def next_column(x):
    y = pltpu.roll(x, LANES - 1, 1)
    lane = lax.broadcasted_iota(jnp.int32, x.shape, 1)
    return jnp.where(lane == LANES - 1, pltpu.roll(y, SUB - 1, 0), y)


def previous_column(x):
    y = pltpu.roll(x, 1, 1)
    lane = lax.broadcasted_iota(jnp.int32, x.shape, 1)
    return jnp.where(lane == 0, pltpu.roll(y, 1, 0), y)


def face(flow, eta_a, eta_b, bed_top, friction):
    hflow = jnp.maximum(jnp.maximum(eta_a, eta_b) - bed_top, depth_floor)
    push = flow - (gravity * time_step / cell_size) * hflow * (eta_b - eta_a)
    drag = 1.0 + friction * jnp.abs(flow) * jnp.exp2(lax.log2(hflow) * (-7.0 / 3.0))
    inverse = pl.reciprocal(drag, approx=True)
    inverse = inverse * (2.0 - drag * inverse)
    return push * inverse


def south_flow(src, bed, row, first, last_row):
    at = row + RIM
    bed_a, bed_b = bed[at, 0], bed[at + 1, 0]
    bed_top = jnp.maximum(bed_a, bed_b)
    friction = bed[at, 1]
    ok = jnp.logical_and(first + row >= 0, first + row < last_row)
    out = []
    for p in range(PARTS):
        eta_a = bed_a + src[3 * at + WATER, p]
        eta_b = bed_b + src[3 * (at + 1) + WATER, p]
        flow = face(src[3 * at + SOUTH, p], eta_a, eta_b, bed_top, friction)
        out.append(jnp.where(ok, flow, 0.0))
    return tuple(out)


def step_rows(src, bed, low, count, unroll, first, last_row, store):
    sub = lax.broadcasted_iota(jnp.int32, (SUB, LANES), 0)
    lane = lax.broadcasted_iota(jnp.int32, (SUB, LANES), 1)
    rim = jnp.logical_and(sub == SUB - 1, lane == LANES - 1)

    def one(i, north):
        row = low + i
        at = row + RIM
        south = south_flow(src, bed, row, first, last_row)
        bed_a = bed[at, 0]
        bed_top = jnp.maximum(bed_a, next_column(bed_a))
        friction = bed[at, 1]
        for p in range(PARTS):
            water = src[3 * at + WATER, p]
            eta = bed_a + water
            east = face(src[3 * at + EAST, p], eta, next_column(eta), bed_top, friction)
            east = jnp.where(rim, 0.0, east)
            west = previous_column(east)
            new = water + (time_step / cell_size) * (west - east + north[p] - south[p])
            store(row, p, EAST, east)
            store(row, p, WATER, new)
            store(row, p, SOUTH, south[p])
        return south

    def some(i, north):
        for k in range(unroll):
            north = one(i * unroll + k, north)
        return north

    north = south_flow(src, bed, low - 1, first, last_row)
    if count == unroll:
        some(0, north)
    else:
        lax.fori_loop(0, count // unroll, some, north)


def keep_in(dst, rim):
    def store(row, p, field, value):
        dst[3 * (row + rim) + field, p] = value

    return store


def exchange_kernel(
    members, slabs,
    water_in, east_in, south_in, bed_in, rough_in, gauges_in, observed_in, ancestors_in,
    state_out, bed_out, lik_out,
    raw, raw_bed, a, b, c, bed, held, held_rim, out, out_rim, pick, slab_lik, sums, far_lik, own_lik,
    gauges, observed, ancestors, in_sem, halo_send, halo_recv, s1, r1, sh, rh, s2, r2, s2h, r2h, ls, lr, fs, fr, ms, mr, own_sem, here_sem,
):
    m = lax.axis_index("member")
    s = lax.axis_index("space")
    up = lax.rem(s + slabs - 1, slabs)
    down = lax.rem(s + 1, slabs)
    across = lax.rem(m + members // 2, members)
    first = s * ROWS
    last_row = slabs * ROWS - 1
    rim_at = m // 2 + 8 * lax.rem(m, 2)
    rim_slot = 1 + rim_at + 48 * (rim_at // 5) + rim_at // 8
    has_up = (s + slabs - 1) // slabs
    has_down = (2 * slabs - 2 - s) // slabs
    holder = [(2 * i if i < 8 else 1, down if i < 5 else up) for i in range(HOLDERS)]

    def remote(src, dst, send, recv, member, slab):
        return pltpu.make_async_remote_copy(
            src_ref=src, dst_ref=dst, send_sem=send, recv_sem=recv,
            device_id=(member, slab), device_id_type=MESH,
        )

    loads = [
        pltpu.make_async_copy(ref, raw.at[i], in_sem.at[i])
        for i, ref in enumerate((east_in, water_in, south_in))
    ] + [
        pltpu.make_async_copy(ref, raw_bed.at[i], in_sem.at[3 + i])
        for i, ref in enumerate((bed_in, rough_in))
    ]
    small = [
        pltpu.make_async_copy(ref, dst, in_sem.at[5 + i])
        for i, (ref, dst) in enumerate(
            ((gauges_in, gauges), (observed_in, observed), (ancestors_in, ancestors))
        )
    ]
    for copy in loads + small:
        copy.start()

    barrier = pltpu.get_barrier_semaphore()

    def greet(member, slab):
        pl.semaphore_signal(barrier, inc=1, device_id=(member, slab), device_id_type=MESH)

    for slab, there in ((up, has_up), (down, has_down)):

        @pl.when(there == 1)
        def _(slab=slab):
            greet(m, slab)
            greet(across, slab)

    @pl.loop(1, members)
    def _(i):
        greet(lax.rem(m + i, members), s)

    for copy in loads:
        copy.wait()

    def lay_out(r):
        from_row = (r // 8) * (8 * SUB) + lax.rem(r, 8)
        for i in range(3):
            for p in range(PARTS):
                a[3 * (r + RIM) + i, p] = raw[i, pl.ds(p * ROWS * SUB + from_row, SUB, stride=8)]
        bed[r + RIM, 0] = raw_bed[0, pl.ds(from_row, SUB, stride=8)]
        rough = raw_bed[1, pl.ds(from_row, SUB, stride=8)]
        bed[r + RIM, 1] = (gravity * time_step) * rough * rough

    @pl.loop(0, RIM)
    def _(r):
        lay_out(r)
        lay_out(ROWS - 1 - r)

    pl.semaphore_wait(barrier, members - 1 + 2 * (has_up + has_down))

    low, high = 3 * RIM, 3 * (RIM + ROWS)
    halos_down = [
        remote(bed.at[pl.ds(ROWS, RIM)], bed.at[pl.ds(0, RIM)], halo_send.at[0], halo_recv.at[0], across, down),
        remote(a.at[pl.ds(high - 5, 5)], a.at[pl.ds(low - 5, 5)], halo_send.at[2], halo_recv.at[2], m, down),
    ]
    halos_up = [
        remote(bed.at[pl.ds(RIM, RIM)], bed.at[pl.ds(RIM + ROWS, RIM)], halo_send.at[1], halo_recv.at[1], across, up),
        remote(a.at[pl.ds(low, 3)], a.at[pl.ds(high, 3)], halo_send.at[3], halo_recv.at[3], m, up),
        remote(a.at[pl.ds(low + 4, 1)], a.at[pl.ds(high + 4, 1)], halo_send.at[4], halo_recv.at[4], m, up),
    ]

    def toward(there, copies, act):
        @pl.when(there == 1)
        def _():
            for copy in copies:
                act(copy)

    toward(has_down, halos_down, lambda copy: copy.start())
    toward(has_up, halos_up, lambda copy: copy.start())

    def announce(t):
        @pl.when(s >= 2**t)
        def _():
            pl.semaphore_signal(here_sem.at[2 * t], inc=1, device_id=(m, s - 2**t), device_id_type=MESH)

        @pl.when(s + 2**t < slabs)
        def _():
            pl.semaphore_signal(here_sem.at[2 * t + 1], inc=1, device_id=(m, s + 2**t), device_id_type=MESH)

    def heard(t):
        @pl.when(s + 2**t < slabs)
        def _():
            pl.semaphore_wait(here_sem.at[2 * t], 1)

        @pl.when(s >= 2**t)
        def _():
            pl.semaphore_wait(here_sem.at[2 * t + 1], 1)

    announce(0)

    @pl.loop(RIM, ROWS - RIM)
    def _(r):
        lay_out(r)

    step_rows(a, bed, 1, ROWS - 2, 7, first, last_row, keep_in(b, RIM))
    step_rows(b, bed, 2, ROWS - 4, 4, first, last_row, keep_in(c, 0))

    heard(0)
    announce(1)

    def spread(to):
        return remote(c.at[pl.ds(3 * to, 3)], held.at[m], s1.at[to], r1.at[m], to, s)

    def spread_from(source):
        return remote(c.at[pl.ds(0, 3)], held.at[source], s1.at[source], r1.at[source], source, s)

    for copy in small:
        copy.wait()

    cell = gauges[...] - first * (SUB * LANES)
    block = cell >> 7
    lane = cell & (LANES - 1)
    count = cell.shape[1]
    blocks = ROWS * SUB
    pick[...] = jnp.where(
        lax.broadcasted_iota(jnp.int32, (blocks, count), 0) == block, 1.0, 0.0
    ).astype(jnp.bfloat16)
    inside = jnp.logical_and(block >= 0, block < blocks)
    here = jnp.logical_and(
        lax.broadcasted_iota(jnp.int32, (LANES, count), 0) == lane, inside
    )

    heard(1)
    announce(2)
    toward(has_up, halos_down, lambda copy: copy.wait_recv())
    toward(has_down, halos_up, lambda copy: copy.wait_recv())
    heard(2)
    announce(3)

    step_rows(a, bed, -1, 2, 2, first, last_row, keep_in(b, RIM))
    step_rows(a, bed, ROWS - 1, 2, 2, first, last_row, keep_in(b, RIM))
    step_rows(b, bed, 0, 2, 2, first, last_row, keep_in(c, 0))
    step_rows(b, bed, ROWS - 2, 2, 2, first, last_row, keep_in(c, 0))

    water = jnp.concatenate(
        [jnp.concatenate([c[3 * r + WATER, p] for r in range(ROWS)], axis=0).T for p in range(PARTS)], axis=0
    )
    value = jnp.zeros((PARTS * LANES, count), jnp.float32)
    for _ in range(3):
        part = water.astype(jnp.bfloat16)
        value += jnp.dot(part, pick[...], preferred_element_type=jnp.float32)
        water = water - part.astype(jnp.float32)
    sub = lax.broadcasted_iota(jnp.int32, (8, LANES), 0)
    at_lane = lax.broadcasted_iota(jnp.int32, (8, LANES), 1)
    tile = jnp.zeros((8, LANES), jnp.float32)
    for p in range(PARTS):
        misfit = jnp.where(here, (value[p * LANES : (p + 1) * LANES] - observed[...]) ** 2, 0.0)
        total = jnp.sum(jnp.sum(misfit, axis=0, keepdims=True), axis=1, keepdims=True)
        spot = jnp.logical_and(sub == s // 4, at_lane == 32 * lax.rem(s, 4) + PARTS * m + p)
        tile = jnp.where(spot, total, tile)
    slab_lik[m] = tile
    twin = s + 1 - 2 * lax.rem(s, 2)

    def share(to):
        return remote(slab_lik.at[m], slab_lik.at[m], ls.at[to], lr.at[m], to, s)

    def share_twin(to):
        return remote(slab_lik.at[m], slab_lik.at[members + m], ls.at[members + to], lr.at[members + m], to, twin)

    @pl.loop(0, members)
    def _(i):
        share_twin(lax.rem(m + i, members)).start()

    @pl.loop(1, members)
    def _(i):
        share(lax.rem(m + i, members)).start()

    @pl.loop(1, members)
    def _(i):
        spread(lax.rem(m + i, members)).start()

    rim_slots = [3 * ROWS - 5 + i for i in range(5)] + [0, 1, 2, 4]
    rims = [
        remote(c.at[rim_slots[i]], held_rim.at[m], sh.at[i], rh.at[m], member, slab)
        for i, (member, slab) in enumerate(holder)
    ]
    toward(has_down, rims[:5], lambda copy: copy.start())
    toward(has_up, rims[5:], lambda copy: copy.start())

    held[m] = c[pl.ds(3 * m, 3)]
    bed_copy = pltpu.make_async_copy(bed, bed_out, own_sem.at[0])
    bed_copy.start()

    def route(to):
        return remote(out.at[to], state_out.at[pl.ds(3 * (m + RIM), 3)], s2.at[to], r2.at[m], to, s)

    def route_from(source):
        return remote(out.at[source], state_out.at[pl.ds(3 * (source + RIM), 3)], s2.at[source], r2.at[source], source, s)

    def route_rim(to):
        return remote(out_rim.at[to], state_out.at[rim_slot], s2h.at[to], r2h.at[rim_at], to, s)

    def wanted(to):
        for k in range(PARTS):
            q = ancestors[PARTS * to + k]
            for f in range(3):
                out[to, f, k] = held[q // PARTS, f, lax.rem(q, PARTS)]

    def wanted_rim(to):
        for k in range(PARTS):
            q = ancestors[PARTS * to + k]
            out_rim[to, k] = held_rim[q // PARTS, lax.rem(q, PARTS)]

    def route_row():
        @pl.loop(1, members)
        def _(i):
            spread_from(lax.rem(m + i, members)).wait_recv()

        @pl.loop(1, members)
        def _(i):
            to = lax.rem(m + i, members)
            wanted(to)
            route(to).start()

        wanted(m)
        pltpu.make_async_copy(out.at[m], state_out.at[pl.ds(3 * (m + RIM), 3)], own_sem.at[1]).start()

    heard(3)
    announce(4)

    @pl.loop(0, members)
    def _(i):
        remote(slab_lik.at[i], slab_lik.at[members + i], ls.at[i], lr.at[members + i], i, twin).wait_recv()

    @pl.loop(1, members)
    def _(i):
        source = lax.rem(m + i, members)
        remote(slab_lik.at[source], slab_lik.at[source], ls.at[source], lr.at[source], source, s).wait_recv()

    tile = slab_lik[0]
    for i in range(1, 2 * members):
        tile = tile + slab_lik[i]
    sums[...] = tile
    heard(4)

    carry = remote(sums, far_lik, fs.at[0], fr.at[0], m, lax.rem(s + 2 * (m + 1), slabs))

    @pl.when(m < members - 1)
    def _():
        carry.start()

    @pl.when(m == members - 1)
    def _():
        far_lik[...] = jnp.zeros((8, LANES), jnp.float32)

    route_row()

    rim_here = jnp.logical_or(
        jnp.logical_and(rim_at < 5, has_up == 1),
        jnp.logical_and(jnp.logical_and(rim_at >= 5, rim_at < HOLDERS), has_down == 1),
    )

    @pl.when(rim_here)
    def _():
        @pl.loop(0, members)
        def _(i):
            remote(c.at[0], held_rim.at[i], sh.at[0], rh.at[i], i, down).wait_recv()

        @pl.loop(1, members)
        def _(i):
            to = lax.rem(m + i, members)
            wanted_rim(to)
            route_rim(to).start()

        wanted_rim(m)
        pltpu.make_async_copy(out_rim.at[m], state_out.at[rim_slot], own_sem.at[2]).start()

    @pl.when(m < members - 1)
    def _():
        carry.wait_recv()

    def tell(to):
        return remote(far_lik, lik_out.at[m], ms.at[to], mr.at[m], to, s)

    @pl.loop(1, members)
    def _(i):
        tell(lax.rem(m + i, members)).start()

    own_lik[...] = far_lik[...] + sums[...]
    mine_lik = pltpu.make_async_copy(own_lik, lik_out.at[m], own_sem.at[3])
    mine_lik.start()

    toward(has_down, halos_down + rims[:5], lambda copy: copy.wait_send())
    toward(has_up, halos_up + rims[5:], lambda copy: copy.wait_send())

    @pl.when(m < members - 1)
    def _():
        carry.wait_send()

    share_twin(m).wait_send()

    @pl.loop(1, members)
    def _(i):
        to = lax.rem(m + i, members)
        spread(to).wait_send()
        route(to).wait_send()
        tell(to).wait_send()
        share(to).wait_send()
        share_twin(to).wait_send()

        @pl.when(rim_here)
        def _():
            route_rim(to).wait_send()

    @pl.loop(1, members)
    def _(i):
        source = lax.rem(m + i, members)
        route_from(source).wait_recv()
        remote(far_lik, lik_out.at[source], ms.at[source], mr.at[source], source, s).wait_recv()

    for i, (member, _) in enumerate(holder):
        slot = 1 + i + 48 * (i // 5) + i // 8

        @pl.when(jnp.logical_and(m != member, (has_up if i < 5 else has_down) == 1))
        def _(i=i, slot=slot, member=member):
            remote(out_rim.at[0], state_out.at[slot], s2h.at[0], r2h.at[i], member, s).wait_recv()

    bed_copy.wait()
    pltpu.make_async_copy(out.at[m], state_out.at[pl.ds(3 * (m + RIM), 3)], own_sem.at[1]).wait()
    mine_lik.wait()

    @pl.when(rim_here)
    def _():
        pltpu.make_async_copy(out_rim.at[m], state_out.at[rim_slot], own_sem.at[2]).wait()


def finish_kernel(
    slabs, state_in, bed_in, lik_in, water_out, east_out, south_out, weight_out,
    a, b, bed, lik, done, in_sem, out_sem,
):
    m = lax.axis_index("member")
    s = lax.axis_index("space")
    first = s * ROWS
    last_row = slabs * ROWS - 1
    half = ROWS // 2
    cut = 3 * (half + 2 * RIM)
    loads = [
        pltpu.make_async_copy(bed_in, bed, in_sem.at[0]),
        pltpu.make_async_copy(state_in.at[pl.ds(0, cut)], a.at[pl.ds(0, cut)], in_sem.at[1]),
        pltpu.make_async_copy(state_in.at[pl.ds(cut, 3 * EXT - cut)], a.at[pl.ds(cut, 3 * EXT - cut)], in_sem.at[2]),
        pltpu.make_async_copy(lik_in, lik, in_sem.at[3]),
    ]
    for copy in loads:
        copy.start()

    def store(row, p, field, value):
        start = p * ROWS * SUB + (row // 8) * (8 * SUB) + lax.rem(row, 8)
        done[field, pl.ds(start, SUB, stride=8)] = value

    copies = []

    def write(part):
        for p in range(PARTS):
            at = pl.ds((2 * p + part) * half * SUB, half * SUB)
            for i, ref in enumerate((east_out, water_out, south_out)):
                copy = pltpu.make_async_copy(done.at[i, at], ref.at[at], out_sem.at[part, p, i])
                copy.start()
                copies.append(copy)

    loads[0].wait()
    loads[1].wait()
    step_rows(a, bed, -1, half + 2, 5, first, last_row, keep_in(b, RIM))
    step_rows(b, bed, 0, half, 4, first, last_row, store)
    write(0)
    loads[2].wait()
    step_rows(a, bed, half + 1, half, 4, first, last_row, keep_in(b, RIM))
    step_rows(b, bed, half, half, 4, first, last_row, store)
    write(1)
    loads[3].wait()

    tile = lik[0]
    for i in range(1, lik.shape[0]):
        tile = tile + lik[i]
    total = jnp.broadcast_to(jnp.sum(tile, axis=0, keepdims=True), tile.shape)
    total = total + pltpu.roll(total, 32, 1)
    total = -0.5 * (total + pltpu.roll(total, 64, 1))
    sub = lax.broadcasted_iota(jnp.int32, total.shape, 0)
    lane = lax.broadcasted_iota(jnp.int32, total.shape, 1)
    once = jnp.logical_and(sub == 0, lane < 32)
    shifted = total - jnp.max(total)
    mass = jnp.sum(jnp.where(once, jnp.exp(shifted), 0.0))
    weights = shifted - jnp.log(jnp.broadcast_to(mass, shifted.shape))
    for p in range(PARTS):
        weight_out[p] = jnp.sum(jnp.where(jnp.logical_and(sub == 0, lane == PARTS * m + p), weights, 0.0))
    for copy in copies:
        copy.wait()


def to_blocks(x):
    lead = x.shape[:-2]
    n = len(lead)
    x = x.reshape(*lead, x.shape[-2] // 8, 8, SUB, LANES)
    x = x.transpose(*range(n), n, n + 2, n + 1, n + 3)
    return x.reshape(-1, LANES)


def from_blocks(x, parts, rows, width):
    x = x.reshape(parts, rows // 8, SUB, 8, LANES).transpose(0, 1, 3, 2, 4)
    return x.reshape(parts, rows, width)


def shards(members, slabs, depth, flow_x, flow_y, terrain, roughness, gauges, observed, ancestors):
    parts, rows, width = depth.shape
    f32 = jnp.float32
    hbm = pl.BlockSpec(memory_space=pl.ANY)
    smem = pl.BlockSpec(memory_space=pltpu.SMEM)
    row = (PARTS, SUB, LANES)
    dma = pltpu.SemaphoreType.DMA
    steps = slabs.bit_length() - 1
    count = gauges.shape[0]
    cells = parts * rows * SUB
    state, bed, lik = pl.pallas_call(
        functools.partial(exchange_kernel, members, slabs),
        out_shape=(
            jax.ShapeDtypeStruct((3 * EXT, *row), f32),
            jax.ShapeDtypeStruct((EXT, 2, SUB, LANES), f32),
            jax.ShapeDtypeStruct((members, 8, LANES), f32),
        ),
        in_specs=[hbm] * 8,
        out_specs=(hbm, hbm, hbm),
        scratch_shapes=[
            pltpu.VMEM((3, cells, LANES), f32),
            pltpu.VMEM((2, rows * SUB, LANES), f32),
            pltpu.VMEM((3 * EXT, *row), f32),
            pltpu.VMEM((3 * EXT, *row), f32),
            pltpu.VMEM((3 * ROWS, *row), f32),
            pltpu.VMEM((EXT, 2, SUB, LANES), f32),
            pltpu.VMEM((members, 3, *row), f32),
            pltpu.VMEM((members, *row), f32),
            pltpu.VMEM((members, 3, *row), f32),
            pltpu.VMEM((members, *row), f32),
            pltpu.VMEM((rows * SUB, count), jnp.bfloat16),
            pltpu.VMEM((2 * members, 8, LANES), f32),
            pltpu.VMEM((8, LANES), f32),
            pltpu.VMEM((8, LANES), f32),
            pltpu.VMEM((8, LANES), f32),
            pltpu.VMEM((1, count), jnp.int32),
            pltpu.VMEM((1, count), f32),
            pltpu.SMEM((members * PARTS,), jnp.int32),
            dma((8,)),
            dma((5,)), dma((5,)),
            dma((members,)), dma((members,)),
            dma((HOLDERS,)), dma((members,)),
            dma((members,)), dma((members,)),
            dma((members,)), dma((HOLDERS,)),
            dma((2 * members,)), dma((2 * members,)),
            dma((1,)), dma((1,)),
            dma((members,)), dma((members,)),
            dma((4,)),
            pltpu.SemaphoreType.REGULAR((2 * steps,)),
        ],
        compiler_params=pltpu.CompilerParams(
            collective_id=0, has_side_effects=True, vmem_limit_bytes=VMEM_LIMIT
        ),
        name="exchange",
    )(
        to_blocks(depth), to_blocks(flow_x), to_blocks(flow_y), to_blocks(terrain), to_blocks(roughness),
        gauges.reshape(1, -1), observed.reshape(1, -1), ancestors,
    )
    water, east, south, weight = pl.pallas_call(
        functools.partial(finish_kernel, slabs),
        out_shape=(jax.ShapeDtypeStruct((cells, LANES), f32),) * 3
        + (jax.ShapeDtypeStruct((parts,), f32),),
        in_specs=[hbm] * 3,
        out_specs=(hbm, hbm, hbm, smem),
        scratch_shapes=[
            pltpu.VMEM((3 * EXT, *row), f32),
            pltpu.VMEM((3 * EXT, *row), f32),
            pltpu.VMEM((EXT, 2, SUB, LANES), f32),
            pltpu.VMEM((members, 8, LANES), f32),
            pltpu.VMEM((3, cells, LANES), f32),
            dma((4,)), dma((2, PARTS, 3)),
        ],
        compiler_params=pltpu.CompilerParams(vmem_limit_bytes=VMEM_LIMIT),
        name="finish",
    )(state, bed, lik)
    back = functools.partial(from_blocks, parts=parts, rows=rows, width=width)
    return back(water), back(east), back(south), weight


def solution(mesh):
    placed = (P("member", "space", None),) * 3 + (P("space", None),) * 2 + (P(),) * 3
    return jax.shard_map(
        functools.partial(shards, mesh.shape["member"], mesh.shape["space"]),
        mesh=mesh,
        in_specs=placed,
        out_specs=(P("member", "space", None),) * 3 + (P("member"),),
        check_vma=False,
    )
```

time: 74.3 us -> 51.8 us (0.70)
  the two profiles are of different devices: /device:TPU:1 before, /device:TPU:65 now
where the time goes in v2:
time: 51.8 us; the launch traced here: 51.7 us
  Pallas kernels  51 us (98%)
  between operations  0.64 us (1%)
    pallas_call x1, Pallas kernels, shards(): pl.pallas_call(functools.partial(exchange_kernel, members, slabs), out_sh...  46.6 us
    pallas_call x1, Pallas kernels, shards(): pl.pallas_call(functools.partial(finish_kernel, slabs), out_shape=(jax.Sh...  4.47 us

profile of v2, /device:TPU:65, one launch (start us, length us, event | category | flops | bytes accessed | tf_op | source)
XLA Modules:
  0.0 51.7 jit_solution(2670342220785554754)
XLA Ops:
  0.6 46.6 %exchange.1 = (f32[60,2,16,128]{3,2,1,0:T(8,128)}, f32[20,2,16,128]{3,2,1,0:T(8,128)}, f32[16,8,128]{2,1,0:T(8,128)}) custom-call(f32[512,128]{1,0:T(8,128)} %bitcast.42, f32[512,128]{1,0:T(8,128)} %bitcast.43, f32[512,128]{1,0:T(8,128)} %bitcast.44, f32[256,128]{1,0:T(8,128)} %bitcast.45, f32[256,128]{1,0:T(8,128)} %bitcast.46, s32[1,512]{1,0:T(1,128)} %bitcast.47, ...), custom_call_target="tpu_custom_call" | custom-call | tf_op jit(solution)/shard_map/exchange/pallas_call | solution.py:544
  47.2 4.5 %finish.1 = (f32[512,128]{1,0:T(8,128)}, f32[512,128]{1,0:T(8,128)}, f32[512,128]{1,0:T(8,128)}, f32[2]{0:T(128)}) custom-call(f32[60,2,16,128]{3,2,1,0:T(8,128)} %get-tuple-element.11.state_in, f32[20,2,16,128]{3,2,1,0:T(8,128)} %get-tuple-element.12.bed_in, f32[16,8,128]{2,1,0:T(8,128)} %get-tuple-element.13.lik_in), custom_call_target="tpu_custom_call" | custom-call | tf_op jit(solution)/shard_map/finish/pallas_call | solution.py:592

commit v3 on v2

--- a/solution.py
+++ b/solution.py
@@ -107,7 +107,7 @@
     members, slabs,
     water_in, east_in, south_in, bed_in, rough_in, gauges_in, observed_in, ancestors_in,
     state_out, bed_out, lik_out,
-    raw, raw_bed, a, b, c, bed, held, held_rim, out, out_rim, pick, slab_lik, sums, far_lik, own_lik,
+    raw, raw_bed, a, b, c, bed, held_a, held_b, held_c, held_rim, out, out_rim, pick, slab_lik, sums, far_lik,
     gauges, observed, ancestors, in_sem, halo_send, halo_recv, s1, r1, sh, rh, s2, r2, s2h, r2h, ls, lr, fs, fr, ms, mr, own_sem, here_sem,
 ):
     m = lax.axis_index("member")
@@ -119,6 +119,7 @@
     last_row = slabs * ROWS - 1
     rim_at = m // 2 + 8 * lax.rem(m, 2)
     rim_slot = 1 + rim_at + 48 * (rim_at // 5) + rim_at // 8
+    held = (held_a, held_b, held_c)
     has_up = (s + slabs - 1) // slabs
     has_down = (2 * slabs - 2 - s) // slabs
     holder = [(2 * i if i < 8 else 1, down if i < 5 else up) for i in range(HOLDERS)]
@@ -230,11 +231,11 @@
     heard(0)
     announce(1)
 
-    def spread(to):
-        return remote(c.at[pl.ds(3 * to, 3)], held.at[m], s1.at[to], r1.at[m], to, s)
-
-    def spread_from(source):
-        return remote(c.at[pl.ds(0, 3)], held.at[source], s1.at[source], r1.at[source], source, s)
+    def spread(to, f):
+        return remote(c.at[3 * to + f], held[f].at[m], s1.at[f, to], r1.at[f, m], to, s)
+
+    def spread_from(source, f):
+        return remote(c.at[f], held[f].at[source], s1.at[f, source], r1.at[f, source], source, s)
 
     for copy in small:
         copy.wait()
@@ -254,10 +255,10 @@
 
     heard(1)
     announce(2)
+    heard(2)
+    announce(3)
     toward(has_up, halos_down, lambda copy: copy.wait_recv())
     toward(has_down, halos_up, lambda copy: copy.wait_recv())
-    heard(2)
-    announce(3)
 
     step_rows(a, bed, -1, 2, 2, first, last_row, keep_in(b, RIM))
     step_rows(a, bed, ROWS - 1, 2, 2, first, last_row, keep_in(b, RIM))
@@ -272,15 +273,13 @@
         part = water.astype(jnp.bfloat16)
         value += jnp.dot(part, pick[...], preferred_element_type=jnp.float32)
         water = water - part.astype(jnp.float32)
-    sub = lax.broadcasted_iota(jnp.int32, (8, LANES), 0)
-    at_lane = lax.broadcasted_iota(jnp.int32, (8, LANES), 1)
-    tile = jnp.zeros((8, LANES), jnp.float32)
+    at_lane = lax.broadcasted_iota(jnp.int32, (1, LANES), 1)
+    entry = jnp.zeros((1, LANES), jnp.float32)
     for p in range(PARTS):
         misfit = jnp.where(here, (value[p * LANES : (p + 1) * LANES] - observed[...]) ** 2, 0.0)
         total = jnp.sum(jnp.sum(misfit, axis=0, keepdims=True), axis=1, keepdims=True)
-        spot = jnp.logical_and(sub == s // 4, at_lane == 32 * lax.rem(s, 4) + PARTS * m + p)
-        tile = jnp.where(spot, total, tile)
-    slab_lik[m] = tile
+        entry = jnp.where(at_lane == 32 * lax.rem(s, 4) + PARTS * m + p, total, entry)
+    slab_lik[m] = entry
     twin = s + 1 - 2 * lax.rem(s, 2)
 
     def share(to):
@@ -297,9 +296,12 @@
     def _(i):
         share(lax.rem(m + i, members)).start()
 
-    @pl.loop(1, members)
-    def _(i):
-        spread(lax.rem(m + i, members)).start()
+    def send_field(f):
+        @pl.loop(1, members)
+        def _(i):
+            spread(lax.rem(m + i, members), f).start()
+
+    send_field(0)
 
     rim_slots = [3 * ROWS - 5 + i for i in range(5)] + [0, 1, 2, 4]
     rims = [
@@ -309,73 +311,86 @@
     toward(has_down, rims[:5], lambda copy: copy.start())
     toward(has_up, rims[5:], lambda copy: copy.start())
 
-    held[m] = c[pl.ds(3 * m, 3)]
-    bed_copy = pltpu.make_async_copy(bed, bed_out, own_sem.at[0])
+    send_field(1)
+    send_field(2)
+    for f in range(3):
+        held[f][m] = c[3 * m + f]
+    bed_copy = pltpu.make_async_copy(bed, bed_out, own_sem.at[6])
     bed_copy.start()
 
-    def route(to):
-        return remote(out.at[to], state_out.at[pl.ds(3 * (m + RIM), 3)], s2.at[to], r2.at[m], to, s)
-
-    def route_from(source):
-        return remote(out.at[source], state_out.at[pl.ds(3 * (source + RIM), 3)], s2.at[source], r2.at[source], source, s)
+    def route(to, f):
+        return remote(out.at[to, f], state_out.at[3 * (m + RIM) + f], s2.at[f, to], r2.at[f, m], to, s)
+
+    def route_from(source, f):
+        return remote(out.at[source, f], state_out.at[3 * (source + RIM) + f], s2.at[f, source], r2.at[f, source], source, s)
 
     def route_rim(to):
         return remote(out_rim.at[to], state_out.at[rim_slot], s2h.at[to], r2h.at[rim_at], to, s)
 
-    def wanted(to):
+    def wanted(to, f):
         for k in range(PARTS):
             q = ancestors[PARTS * to + k]
-            for f in range(3):
-                out[to, f, k] = held[q // PARTS, f, lax.rem(q, PARTS)]
+            out[to, f, k] = held[f][q // PARTS, lax.rem(q, PARTS)]
 
     def wanted_rim(to):
         for k in range(PARTS):
             q = ancestors[PARTS * to + k]
             out_rim[to, k] = held_rim[q // PARTS, lax.rem(q, PARTS)]
 
-    def route_row():
+    def mine(f):
+        return pltpu.make_async_copy(out.at[m, f], state_out.at[3 * (m + RIM) + f], own_sem.at[f])
+
+    def route_field(f):
         @pl.loop(1, members)
         def _(i):
-            spread_from(lax.rem(m + i, members)).wait_recv()
+            spread_from(lax.rem(m + i, members), f).wait_recv()
 
         @pl.loop(1, members)
         def _(i):
             to = lax.rem(m + i, members)
-            wanted(to)
-            route(to).start()
-
-        wanted(m)
-        pltpu.make_async_copy(out.at[m], state_out.at[pl.ds(3 * (m + RIM), 3)], own_sem.at[1]).start()
+            wanted(to, f)
+            route(to, f).start()
+
+        wanted(m, f)
+        mine(f).start()
 
     heard(3)
     announce(4)
 
-    @pl.loop(0, members)
-    def _(i):
-        remote(slab_lik.at[i], slab_lik.at[members + i], ls.at[i], lr.at[members + i], i, twin).wait_recv()
-
-    @pl.loop(1, members)
-    def _(i):
-        source = lax.rem(m + i, members)
-        remote(slab_lik.at[source], slab_lik.at[source], ls.at[source], lr.at[source], source, s).wait_recv()
-
-    tile = slab_lik[0]
-    for i in range(1, 2 * members):
-        tile = tile + slab_lik[i]
-    sums[...] = tile
-    heard(4)
-
     carry = remote(sums, far_lik, fs.at[0], fr.at[0], m, lax.rem(s + 2 * (m + 1), slabs))
 
-    @pl.when(m < members - 1)
+    def carry_sums():
+        @pl.loop(0, members)
+        def _(i):
+            remote(slab_lik.at[i], slab_lik.at[members + i], ls.at[i], lr.at[members + i], i, twin).wait_recv()
+
+        @pl.loop(1, members)
+        def _(i):
+            source = lax.rem(m + i, members)
+            remote(slab_lik.at[source], slab_lik.at[source], ls.at[source], lr.at[source], source, s).wait_recv()
+
+        entry = slab_lik[0]
+        for i in range(1, 2 * members):
+            entry = entry + slab_lik[i]
+        sums[...] = entry
+        heard(4)
+
+        @pl.when(m < members - 1)
+        def _():
+            carry.start()
+
+    @pl.when(s >= slabs // 2)
     def _():
-        carry.start()
-
-    @pl.when(m == members - 1)
+        carry_sums()
+
+    route_field(0)
+
+    @pl.when(s < slabs // 2)
     def _():
-        far_lik[...] = jnp.zeros((8, LANES), jnp.float32)
-
-    route_row()
+        carry_sums()
+
+    route_field(1)
+    route_field(2)
 
     rim_here = jnp.logical_or(
         jnp.logical_and(rim_at < 5, has_up == 1),
@@ -395,21 +410,22 @@
             route_rim(to).start()
 
         wanted_rim(m)
-        pltpu.make_async_copy(out_rim.at[m], state_out.at[rim_slot], own_sem.at[2]).start()
+        pltpu.make_async_copy(out_rim.at[m], state_out.at[rim_slot], own_sem.at[3]).start()
+
+    def tell(to):
+        return remote(far_lik, lik_out.at[m], ms.at[to], mr.at[m], to, s)
 
     @pl.when(m < members - 1)
     def _():
         carry.wait_recv()
 
-    def tell(to):
-        return remote(far_lik, lik_out.at[m], ms.at[to], mr.at[m], to, s)
-
-    @pl.loop(1, members)
-    def _(i):
-        tell(lax.rem(m + i, members)).start()
-
-    own_lik[...] = far_lik[...] + sums[...]
-    mine_lik = pltpu.make_async_copy(own_lik, lik_out.at[m], own_sem.at[3])
+        @pl.loop(1, members)
+        def _(i):
+            tell(lax.rem(m + i, members)).start()
+
+        pltpu.make_async_copy(far_lik, lik_out.at[m], own_sem.at[4]).start()
+
+    mine_lik = pltpu.make_async_copy(sums, lik_out.at[members - 1], own_sem.at[5])
     mine_lik.start()
 
     toward(has_down, halos_down + rims[:5], lambda copy: copy.wait_send())
@@ -418,15 +434,20 @@
     @pl.when(m < members - 1)
     def _():
         carry.wait_send()
+        pltpu.make_async_copy(far_lik, lik_out.at[m], own_sem.at[4]).wait()
+
+        @pl.loop(1, members)
+        def _(i):
+            tell(lax.rem(m + i, members)).wait_send()
 
     share_twin(m).wait_send()
 
     @pl.loop(1, members)
     def _(i):
         to = lax.rem(m + i, members)
-        spread(to).wait_send()
-        route(to).wait_send()
-        tell(to).wait_send()
+        for f in range(3):
+            spread(to, f).wait_send()
+            route(to, f).wait_send()
         share(to).wait_send()
         share_twin(to).wait_send()
 
@@ -437,8 +458,12 @@
     @pl.loop(1, members)
     def _(i):
         source = lax.rem(m + i, members)
-        route_from(source).wait_recv()
-        remote(far_lik, lik_out.at[source], ms.at[source], mr.at[source], source, s).wait_recv()
+        for f in range(3):
+            route_from(source, f).wait_recv()
+
+        @pl.when(source < members - 1)
+        def _():
+            remote(far_lik, lik_out.at[source], ms.at[source], mr.at[source], source, s).wait_recv()
 
     for i, (member, _) in enumerate(holder):
         slot = 1 + i + 48 * (i // 5) + i // 8
@@ -448,12 +473,13 @@
             remote(out_rim.at[0], state_out.at[slot], s2h.at[0], r2h.at[i], member, s).wait_recv()
 
     bed_copy.wait()
-    pltpu.make_async_copy(out.at[m], state_out.at[pl.ds(3 * (m + RIM), 3)], own_sem.at[1]).wait()
+    for f in range(3):
+        mine(f).wait()
     mine_lik.wait()
 
     @pl.when(rim_here)
     def _():
-        pltpu.make_async_copy(out_rim.at[m], state_out.at[rim_slot], own_sem.at[2]).wait()
+        pltpu.make_async_copy(out_rim.at[m], state_out.at[rim_slot], own_sem.at[3]).wait()
 
 
 def finish_kernel(
@@ -500,9 +526,12 @@
     write(1)
     loads[3].wait()
 
-    tile = lik[0]
-    for i in range(1, lik.shape[0]):
-        tile = tile + lik[i]
+    members = lik.shape[0]
+    at_slab = lax.broadcasted_iota(jnp.int32, (8, LANES), 0)
+    tile = jnp.zeros((8, LANES), jnp.float32)
+    for i in range(members):
+        source = lax.rem(s + 2 * slabs - 2 * (i + 1), slabs)
+        tile = tile + jnp.where(at_slab == source // 4, lik[i], 0.0)
     total = jnp.broadcast_to(jnp.sum(tile, axis=0, keepdims=True), tile.shape)
     total = total + pltpu.roll(total, 32, 1)
     total = -0.5 * (total + pltpu.roll(total, 64, 1))
@@ -546,7 +575,7 @@
         out_shape=(
             jax.ShapeDtypeStruct((3 * EXT, *row), f32),
             jax.ShapeDtypeStruct((EXT, 2, SUB, LANES), f32),
-            jax.ShapeDtypeStruct((members, 8, LANES), f32),
+            jax.ShapeDtypeStruct((members, 1, LANES), f32),
         ),
         in_specs=[hbm] * 8,
         out_specs=(hbm, hbm, hbm),
@@ -557,28 +586,29 @@
             pltpu.VMEM((3 * EXT, *row), f32),
             pltpu.VMEM((3 * ROWS, *row), f32),
             pltpu.VMEM((EXT, 2, SUB, LANES), f32),
-            pltpu.VMEM((members, 3, *row), f32),
+            pltpu.VMEM((members, *row), f32),
+            pltpu.VMEM((members, *row), f32),
+            pltpu.VMEM((members, *row), f32),
             pltpu.VMEM((members, *row), f32),
             pltpu.VMEM((members, 3, *row), f32),
             pltpu.VMEM((members, *row), f32),
             pltpu.VMEM((rows * SUB, count), jnp.bfloat16),
-            pltpu.VMEM((2 * members, 8, LANES), f32),
-            pltpu.VMEM((8, LANES), f32),
-            pltpu.VMEM((8, LANES), f32),
-            pltpu.VMEM((8, LANES), f32),
+            pltpu.VMEM((2 * members, 1, LANES), f32),
+            pltpu.VMEM((1, LANES), f32),
+            pltpu.VMEM((1, LANES), f32),
             pltpu.VMEM((1, count), jnp.int32),
             pltpu.VMEM((1, count), f32),
             pltpu.SMEM((members * PARTS,), jnp.int32),
             dma((8,)),
             dma((5,)), dma((5,)),
-            dma((members,)), dma((members,)),
+            dma((3, members)), dma((3, members)),
             dma((HOLDERS,)), dma((members,)),
-            dma((members,)), dma((members,)),
+            dma((3, members)), dma((3, members)),
             dma((members,)), dma((HOLDERS,)),
             dma((2 * members,)), dma((2 * members,)),
             dma((1,)), dma((1,)),
             dma((members,)), dma((members,)),
-            dma((4,)),
+            dma((7,)),
             pltpu.SemaphoreType.REGULAR((2 * steps,)),
         ],
         compiler_params=pltpu.CompilerParams(
@@ -599,7 +629,7 @@
             pltpu.VMEM((3 * EXT, *row), f32),
             pltpu.VMEM((3 * EXT, *row), f32),
             pltpu.VMEM((EXT, 2, SUB, LANES), f32),
-            pltpu.VMEM((members, 8, LANES), f32),
+            pltpu.VMEM((members, 1, LANES), f32),
             pltpu.VMEM((3, cells, LANES), f32),
             dma((4,)), dma((2, PARTS, 3)),
         ],

time: 51.8 us -> 48.5 us (0.936)
  the two profiles are of different devices: /device:TPU:65 before, /device:TPU:1 now
where the time goes in v3:
time: 48.5 us; the launch traced here: 48.3 us
  Pallas kernels  47.6 us (98%)
  between operations  0.64 us (1%)
    pallas_call x1, Pallas kernels, shards(): pl.pallas_call(functools.partial(exchange_kernel, members, slabs), out_sh...  43.2 us
    pallas_call x1, Pallas kernels, shards(): pl.pallas_call(functools.partial(finish_kernel, slabs), out_shape=(jax.Sh...  4.47 us

profile of v3, /device:TPU:1, one launch (start us, length us, event | category | flops | bytes accessed | tf_op | source)
XLA Modules:
  0.0 48.3 jit_solution(31005192961944928)
XLA Ops:
  0.6 43.2 %exchange.1 = (f32[60,2,16,128]{3,2,1,0:T(8,128)}, f32[20,2,16,128]{3,2,1,0:T(8,128)}, f32[16,1,128]{2,1,0:T(1,128)}) custom-call(f32[512,128]{1,0:T(8,128)} %bitcast.42, f32[512,128]{1,0:T(8,128)} %bitcast.43, f32[512,128]{1,0:T(8,128)} %bitcast.44, f32[256,128]{1,0:T(8,128)} %bitcast.45, f32[256,128]{1,0:T(8,128)} %bitcast.46, s32[1,512]{1,0:T(1,128)} %bitcast.47, ...), custom_call_target="tpu_custom_call" | custom-call | tf_op jit(solution)/shard_map/exchange/pallas_call | solution.py:573
  43.8 4.5 %finish.1 = (f32[512,128]{1,0:T(8,128)}, f32[512,128]{1,0:T(8,128)}, f32[512,128]{1,0:T(8,128)}, f32[2]{0:T(128)}) custom-call(f32[60,2,16,128]{3,2,1,0:T(8,128)} %get-tuple-element.11.state_in, f32[20,2,16,128]{3,2,1,0:T(8,128)} %get-tuple-element.12.bed_in, f32[16,1,128]{2,1,0:T(1,128)} %get-tuple-element.13.lik_in), custom_call_target="tpu_custom_call" | custom-call | tf_op jit(solution)/shard_map/finish/pallas_call | solution.py:622

commit v4 on v3

--- a/solution.py
+++ b/solution.py
@@ -107,8 +107,8 @@
     members, slabs,
     water_in, east_in, south_in, bed_in, rough_in, gauges_in, observed_in, ancestors_in,
     state_out, bed_out, lik_out,
-    raw, raw_bed, a, b, c, bed, held_a, held_b, held_c, held_rim, out, out_rim, pick, slab_lik, sums, far_lik,
-    gauges, observed, ancestors, in_sem, halo_send, halo_recv, s1, r1, sh, rh, s2, r2, s2h, r2h, ls, lr, fs, fr, ms, mr, own_sem, here_sem,
+    raw, raw_bed, a, b, c, bed, held_a, held_b, held_c, held_rim, out, out_rim, pick, z_lik, sums,
+    gauges, observed, ancestors, in_sem, halo_send, halo_recv, s1, r1, sh, rh, s2, r2, s2h, r2h, ls, lr, ms, mr, own_sem, here_sem,
 ):
     m = lax.axis_index("member")
     s = lax.axis_index("space")
@@ -232,10 +232,13 @@
     announce(1)
 
     def spread(to, f):
-        return remote(c.at[3 * to + f], held[f].at[m], s1.at[f, to], r1.at[f, m], to, s)
-
-    def spread_from(source, f):
-        return remote(c.at[f], held[f].at[source], s1.at[f, source], r1.at[f, source], source, s)
+        return remote(c.at[3 * to + f], held[f].at[m], s1.at[f], r1.at[f], to, s)
+
+    def batch(src, dst, count, send, recv):
+        return remote(src.at[pl.ds(0, count)], dst.at[pl.ds(0, count)], send, recv, across, s)
+
+    def spread_all(f):
+        return batch(c, held[f], members - 1, s1.at[f], r1.at[f])
 
     for copy in small:
         copy.wait()
@@ -264,6 +267,26 @@
     step_rows(a, bed, ROWS - 1, 2, 2, first, last_row, keep_in(b, RIM))
     step_rows(b, bed, 0, 2, 2, first, last_row, keep_in(c, 0))
     step_rows(b, bed, ROWS - 2, 2, 2, first, last_row, keep_in(c, 0))
+
+    def send_field(f):
+        @pl.loop(1, members)
+        def _(i):
+            spread(lax.rem(m + i, members), f).start()
+
+    send_field(0)
+
+    rim_slots = [3 * ROWS - 5 + i for i in range(5)] + [0, 1, 2, 4]
+    rims = [
+        remote(c.at[rim_slots[i]], held_rim.at[m], sh.at[i // 5], rh.at[0], member, slab)
+        for i, (member, slab) in enumerate(holder)
+    ]
+    toward(has_down, rims[:5], lambda copy: copy.start())
+    toward(has_up, rims[5:], lambda copy: copy.start())
+
+    send_field(1)
+    send_field(2)
+    heard(3)
+    announce(4)
 
     water = jnp.concatenate(
         [jnp.concatenate([c[3 * r + WATER, p] for r in range(ROWS)], axis=0).T for p in range(PARTS)], axis=0
@@ -278,54 +301,33 @@
     for p in range(PARTS):
         misfit = jnp.where(here, (value[p * LANES : (p + 1) * LANES] - observed[...]) ** 2, 0.0)
         total = jnp.sum(jnp.sum(misfit, axis=0, keepdims=True), axis=1, keepdims=True)
-        entry = jnp.where(at_lane == 32 * lax.rem(s, 4) + PARTS * m + p, total, entry)
-    slab_lik[m] = entry
-    twin = s + 1 - 2 * lax.rem(s, 2)
-
-    def share(to):
-        return remote(slab_lik.at[m], slab_lik.at[m], ls.at[to], lr.at[m], to, s)
-
-    def share_twin(to):
-        return remote(slab_lik.at[m], slab_lik.at[members + m], ls.at[members + to], lr.at[members + m], to, twin)
-
-    @pl.loop(0, members)
-    def _(i):
-        share_twin(lax.rem(m + i, members)).start()
-
-    @pl.loop(1, members)
-    def _(i):
-        share(lax.rem(m + i, members)).start()
-
-    def send_field(f):
-        @pl.loop(1, members)
+        entry = jnp.where(at_lane == PARTS * s + p, total, entry)
+    z = s // 2
+    z_lik[z] = entry
+
+    def share(i):
+        return remote(z_lik.at[z], z_lik.at[z], ls.at[0], lr.at[0], m, lax.rem(s + 2 * i, slabs))
+
+    def share_all():
+        heard(4)
+
+        @pl.loop(1, slabs // 2)
         def _(i):
-            spread(lax.rem(m + i, members), f).start()
-
-    send_field(0)
-
-    rim_slots = [3 * ROWS - 5 + i for i in range(5)] + [0, 1, 2, 4]
-    rims = [
-        remote(c.at[rim_slots[i]], held_rim.at[m], sh.at[i], rh.at[m], member, slab)
-        for i, (member, slab) in enumerate(holder)
-    ]
-    toward(has_down, rims[:5], lambda copy: copy.start())
-    toward(has_up, rims[5:], lambda copy: copy.start())
-
-    send_field(1)
-    send_field(2)
+            share(i).start()
+
     for f in range(3):
         held[f][m] = c[3 * m + f]
     bed_copy = pltpu.make_async_copy(bed, bed_out, own_sem.at[6])
     bed_copy.start()
 
     def route(to, f):
-        return remote(out.at[to, f], state_out.at[3 * (m + RIM) + f], s2.at[f, to], r2.at[f, m], to, s)
-
-    def route_from(source, f):
-        return remote(out.at[source, f], state_out.at[3 * (source + RIM) + f], s2.at[f, source], r2.at[f, source], source, s)
+        return remote(out.at[to, f], state_out.at[3 * (m + RIM) + f], s2.at[f], r2.at[f], to, s)
+
+    def route_all(f):
+        return batch(c, state_out, members - 1, s2.at[f], r2.at[f])
 
     def route_rim(to):
-        return remote(out_rim.at[to], state_out.at[rim_slot], s2h.at[to], r2h.at[rim_at], to, s)
+        return remote(out_rim.at[to], state_out.at[rim_slot], s2h.at[0], r2h.at[rim_at], to, s)
 
     def wanted(to, f):
         for k in range(PARTS):
@@ -341,9 +343,7 @@
         return pltpu.make_async_copy(out.at[m, f], state_out.at[3 * (m + RIM) + f], own_sem.at[f])
 
     def route_field(f):
-        @pl.loop(1, members)
-        def _(i):
-            spread_from(lax.rem(m + i, members), f).wait_recv()
+        spread_all(f).wait_recv()
 
         @pl.loop(1, members)
         def _(i):
@@ -354,42 +354,15 @@
         wanted(m, f)
         mine(f).start()
 
-    heard(3)
-    announce(4)
-
-    carry = remote(sums, far_lik, fs.at[0], fr.at[0], m, lax.rem(s + 2 * (m + 1), slabs))
-
-    def carry_sums():
-        @pl.loop(0, members)
-        def _(i):
-            remote(slab_lik.at[i], slab_lik.at[members + i], ls.at[i], lr.at[members + i], i, twin).wait_recv()
-
-        @pl.loop(1, members)
-        def _(i):
-            source = lax.rem(m + i, members)
-            remote(slab_lik.at[source], slab_lik.at[source], ls.at[source], lr.at[source], source, s).wait_recv()
-
-        entry = slab_lik[0]
-        for i in range(1, 2 * members):
-            entry = entry + slab_lik[i]
-        sums[...] = entry
-        heard(4)
-
-        @pl.when(m < members - 1)
-        def _():
-            carry.start()
-
-    @pl.when(s >= slabs // 2)
+
+    @pl.when(s >= slabs // 4)
     def _():
-        carry_sums()
+        share_all()
 
     route_field(0)
 
-    @pl.when(s < slabs // 2)
-    def _():
-        carry_sums()
-
     route_field(1)
+
     route_field(2)
 
     rim_here = jnp.logical_or(
@@ -399,9 +372,7 @@
 
     @pl.when(rim_here)
     def _():
-        @pl.loop(0, members)
-        def _(i):
-            remote(c.at[0], held_rim.at[i], sh.at[0], rh.at[i], i, down).wait_recv()
+        batch(c, held_rim, members, sh.at[0], rh.at[0]).wait_recv()
 
         @pl.loop(1, members)
         def _(i):
@@ -412,65 +383,60 @@
         wanted_rim(m)
         pltpu.make_async_copy(out_rim.at[m], state_out.at[rim_slot], own_sem.at[3]).start()
 
+    @pl.when(s < slabs // 4)
+    def _():
+        share_all()
+
+    share_batch = batch(z_lik, z_lik, slabs // 2 - 1, ls.at[0], lr.at[0])
+    share_batch.wait_recv()
+    entry = z_lik[0]
+    for i in range(1, slabs // 2):
+        entry = entry + z_lik[i]
+    sums[...] = entry
+    side = members * lax.rem(s, 2)
+    twin = s + 1 - 2 * lax.rem(s, 2)
+
     def tell(to):
-        return remote(far_lik, lik_out.at[m], ms.at[to], mr.at[m], to, s)
-
-    @pl.when(m < members - 1)
-    def _():
-        carry.wait_recv()
-
-        @pl.loop(1, members)
-        def _(i):
-            tell(lax.rem(m + i, members)).start()
-
-        pltpu.make_async_copy(far_lik, lik_out.at[m], own_sem.at[4]).start()
-
-    mine_lik = pltpu.make_async_copy(sums, lik_out.at[members - 1], own_sem.at[5])
-    mine_lik.start()
-
-    toward(has_down, halos_down + rims[:5], lambda copy: copy.wait_send())
-    toward(has_up, halos_up + rims[5:], lambda copy: copy.wait_send())
-
-    @pl.when(m < members - 1)
-    def _():
-        carry.wait_send()
-        pltpu.make_async_copy(far_lik, lik_out.at[m], own_sem.at[4]).wait()
-
-        @pl.loop(1, members)
-        def _(i):
-            tell(lax.rem(m + i, members)).wait_send()
-
-    share_twin(m).wait_send()
+        return remote(sums, lik_out.at[side + m], ms.at[0], mr.at[0], to, s)
+
+    def tell_twin(to):
+        return remote(sums, lik_out.at[side + m], ms.at[0], mr.at[0], to, twin)
+
+    @pl.loop(0, members)
+    def _(i):
+        tell_twin(lax.rem(m + i, members)).start()
 
     @pl.loop(1, members)
     def _(i):
-        to = lax.rem(m + i, members)
-        for f in range(3):
-            spread(to, f).wait_send()
-            route(to, f).wait_send()
-        share(to).wait_send()
-        share_twin(to).wait_send()
-
-        @pl.when(rim_here)
-        def _():
-            route_rim(to).wait_send()
-
-    @pl.loop(1, members)
-    def _(i):
-        source = lax.rem(m + i, members)
-        for f in range(3):
-            route_from(source, f).wait_recv()
-
-        @pl.when(source < members - 1)
-        def _():
-            remote(far_lik, lik_out.at[source], ms.at[source], mr.at[source], source, s).wait_recv()
+        tell(lax.rem(m + i, members)).start()
+
+    mine_lik = pltpu.make_async_copy(sums, lik_out.at[side + m], own_sem.at[5])
+    mine_lik.start()
+
+    toward(has_down, halos_down + [batch(c, held_rim, 5, sh.at[0], rh.at[0])], lambda copy: copy.wait_send())
+    toward(has_up, halos_up + [batch(c, held_rim, 4, sh.at[1], rh.at[0])], lambda copy: copy.wait_send())
+
+    tell_batch = batch(lik_out, lik_out, 2 * members - 1, ms.at[0], mr.at[0])
+    share_batch.wait_send()
+    tell_batch.wait_send()
+    for f in range(3):
+        spread_all(f).wait_send()
+        route_all(f).wait_send()
+
+    @pl.when(rim_here)
+    def _():
+        batch(c, held_rim, members - 1, s2h.at[0], rh.at[0]).wait_send()
+
+    for f in range(3):
+        route_all(f).wait_recv()
+    tell_batch.wait_recv()
 
     for i, (member, _) in enumerate(holder):
         slot = 1 + i + 48 * (i // 5) + i // 8
 
         @pl.when(jnp.logical_and(m != member, (has_up if i < 5 else has_down) == 1))
         def _(i=i, slot=slot, member=member):
-            remote(out_rim.at[0], state_out.at[slot], s2h.at[0], r2h.at[i], member, s).wait_recv()
+            remote(out_rim.at[0], state_out.at[slot], s2h.at[0], r2h.at[i], across, s).wait_recv()
 
     bed_copy.wait()
     for f in range(3):
@@ -498,7 +464,7 @@
         pltpu.make_async_copy(state_in.at[pl.ds(cut, 3 * EXT - cut)], a.at[pl.ds(cut, 3 * EXT - cut)], in_sem.at[2]),
         pltpu.make_async_copy(lik_in, lik, in_sem.at[3]),
     ]
-    for copy in loads:
+    for copy in loads[3:] + loads[:3]:
         copy.start()
 
     def store(row, p, field, value):
@@ -515,6 +481,23 @@
                 copy.start()
                 copies.append(copy)
 
+    loads[3].wait()
+
+    members = lik.shape[0] // 2
+    rows = lik[0:members] + lik[members : 2 * members]
+    own = lax.broadcasted_iota(jnp.int32, rows.shape, 0) == m
+    lane = lax.broadcasted_iota(jnp.int32, rows.shape, 2)
+    totals = []
+    for p in range(PARTS):
+        total = jnp.sum(jnp.where(lax.rem(lane, PARTS) == p, rows, 0.0), axis=2, keepdims=True)
+        totals.append(-0.5 * jnp.broadcast_to(total, rows.shape))
+    top = jnp.max(functools.reduce(jnp.maximum, totals))
+    once = lane == 0
+    mass = jnp.sum(jnp.where(once, sum(jnp.exp(total - top) for total in totals), 0.0))
+    log_mass = jnp.log(jnp.broadcast_to(mass, rows.shape))
+    for p in range(PARTS):
+        weights = totals[p] - top - log_mass
+        weight_out[p] = jnp.sum(jnp.where(jnp.logical_and(own, once), weights, 0.0))
     loads[0].wait()
     loads[1].wait()
     step_rows(a, bed, -1, half + 2, 5, first, last_row, keep_in(b, RIM))
@@ -524,25 +507,6 @@
     step_rows(a, bed, half + 1, half, 4, first, last_row, keep_in(b, RIM))
     step_rows(b, bed, half, half, 4, first, last_row, store)
     write(1)
-    loads[3].wait()
-
-    members = lik.shape[0]
-    at_slab = lax.broadcasted_iota(jnp.int32, (8, LANES), 0)
-    tile = jnp.zeros((8, LANES), jnp.float32)
-    for i in range(members):
-        source = lax.rem(s + 2 * slabs - 2 * (i + 1), slabs)
-        tile = tile + jnp.where(at_slab == source // 4, lik[i], 0.0)
-    total = jnp.broadcast_to(jnp.sum(tile, axis=0, keepdims=True), tile.shape)
-    total = total + pltpu.roll(total, 32, 1)
-    total = -0.5 * (total + pltpu.roll(total, 64, 1))
-    sub = lax.broadcasted_iota(jnp.int32, total.shape, 0)
-    lane = lax.broadcasted_iota(jnp.int32, total.shape, 1)
-    once = jnp.logical_and(sub == 0, lane < 32)
-    shifted = total - jnp.max(total)
-    mass = jnp.sum(jnp.where(once, jnp.exp(shifted), 0.0))
-    weights = shifted - jnp.log(jnp.broadcast_to(mass, shifted.shape))
-    for p in range(PARTS):
-        weight_out[p] = jnp.sum(jnp.where(jnp.logical_and(sub == 0, lane == PARTS * m + p), weights, 0.0))
     for copy in copies:
         copy.wait()
 
@@ -575,7 +539,7 @@
         out_shape=(
             jax.ShapeDtypeStruct((3 * EXT, *row), f32),
             jax.ShapeDtypeStruct((EXT, 2, SUB, LANES), f32),
-            jax.ShapeDtypeStruct((members, 1, LANES), f32),
+            jax.ShapeDtypeStruct((2 * members, 1, LANES), f32),
         ),
         in_specs=[hbm] * 8,
         out_specs=(hbm, hbm, hbm),
@@ -593,21 +557,19 @@
             pltpu.VMEM((members, 3, *row), f32),
             pltpu.VMEM((members, *row), f32),
             pltpu.VMEM((rows * SUB, count), jnp.bfloat16),
-            pltpu.VMEM((2 * members, 1, LANES), f32),
-            pltpu.VMEM((1, LANES), f32),
+            pltpu.VMEM((slabs // 2, 1, LANES), f32),
             pltpu.VMEM((1, LANES), f32),
             pltpu.VMEM((1, count), jnp.int32),
             pltpu.VMEM((1, count), f32),
             pltpu.SMEM((members * PARTS,), jnp.int32),
             dma((8,)),
             dma((5,)), dma((5,)),
-            dma((3, members)), dma((3, members)),
-            dma((HOLDERS,)), dma((members,)),
-            dma((3, members)), dma((3, members)),
-            dma((members,)), dma((HOLDERS,)),
-            dma((2 * members,)), dma((2 * members,)),
+            dma((3,)), dma((3,)),
+            dma((2,)), dma((1,)),
+            dma((3,)), dma((3,)),
+            dma((1,)), dma((HOLDERS,)),
             dma((1,)), dma((1,)),
-            dma((members,)), dma((members,)),
+            dma((1,)), dma((1,)),
             dma((7,)),
             pltpu.SemaphoreType.REGULAR((2 * steps,)),
         ],
@@ -629,7 +591,7 @@
             pltpu.VMEM((3 * EXT, *row), f32),
             pltpu.VMEM((3 * EXT, *row), f32),
             pltpu.VMEM((EXT, 2, SUB, LANES), f32),
-            pltpu.VMEM((members, 1, LANES), f32),
+            pltpu.VMEM((2 * members, 1, LANES), f32),
             pltpu.VMEM((3, cells, LANES), f32),
             dma((4,)), dma((2, PARTS, 3)),
         ],

time: 48.5 us -> 47.1 us (0.971)
  Pallas kernels: 47.6 us -> 46.2 us
    pallas_call x1, Pallas kernels: 43.2 us -> 41.7 us  [shards(): pl.pallas_call(functools.partial(exchange_kernel, members, slabs), out_sh...]
where the time goes in v4:
time: 47.1 us; the launch traced here: 46.9 us
  Pallas kernels  46.2 us (98%)
  between operations  0.64 us (1%)
    pallas_call x1, Pallas kernels, shards(): pl.pallas_call(functools.partial(exchange_kernel, members, slabs), out_sh...  41.7 us
    pallas_call x1, Pallas kernels, shards(): pl.pallas_call(functools.partial(finish_kernel, slabs), out_shape=(jax.Sh...  4.49 us

profile of v4, /device:TPU:1, one launch (start us, length us, event | category | flops | bytes accessed | tf_op | source)
XLA Modules:
  0.0 46.9 jit_solution(12826832145858247889)
XLA Ops:
  0.6 41.7 %exchange.1 = (f32[60,2,16,128]{3,2,1,0:T(8,128)}, f32[20,2,16,128]{3,2,1,0:T(8,128)}, f32[32,1,128]{2,1,0:T(1,128)}) custom-call(f32[512,128]{1,0:T(8,128)} %bitcast.42, f32[512,128]{1,0:T(8,128)} %bitcast.43, f32[512,128]{1,0:T(8,128)} %bitcast.44, f32[256,128]{1,0:T(8,128)} %bitcast.45, f32[256,128]{1,0:T(8,128)} %bitcast.46, s32[1,512]{1,0:T(1,128)} %bitcast.47, ...), custom_call_target="tpu_custom_call" | custom-call | tf_op jit(solution)/shard_map/exchange/pallas_call | solution.py:537
  42.4 4.5 %finish.1 = (f32[512,128]{1,0:T(8,128)}, f32[512,128]{1,0:T(8,128)}, f32[512,128]{1,0:T(8,128)}, f32[2]{0:T(128)}) custom-call(f32[60,2,16,128]{3,2,1,0:T(8,128)} %get-tuple-element.11.state_in, f32[20,2,16,128]{3,2,1,0:T(8,128)} %get-tuple-element.12.bed_in, f32[32,1,128]{2,1,0:T(1,128)} %get-tuple-element.13.lik_in), custom_call_target="tpu_custom_call" | custom-call | tf_op jit(solution)/shard_map/finish/pallas_call | solution.py:584

commit v5 on v4

--- a/solution.py
+++ b/solution.py
@@ -258,8 +258,14 @@
 
     heard(1)
     announce(2)
-    heard(2)
-    announce(3)
+    def third():
+        heard(2)
+        announce(3)
+
+    @pl.when(s >= slabs // 4)
+    def _():
+        third()
+
     toward(has_up, halos_down, lambda copy: copy.wait_recv())
     toward(has_down, halos_up, lambda copy: copy.wait_recv())
 
@@ -272,6 +278,14 @@
         @pl.loop(1, members)
         def _(i):
             spread(lax.rem(m + i, members), f).start()
+
+    def fourth():
+        heard(3)
+        announce(4)
+
+    @pl.when(s >= slabs // 2)
+    def _():
+        fourth()
 
     send_field(0)
 
@@ -285,8 +299,14 @@
 
     send_field(1)
     send_field(2)
-    heard(3)
-    announce(4)
+    @pl.when(s < slabs // 4)
+    def _():
+        third()
+
+    @pl.when(s < slabs // 2)
+    def _():
+        fourth()
+
 
     water = jnp.concatenate(
         [jnp.concatenate([c[3 * r + WATER, p] for r in range(ROWS)], axis=0).T for p in range(PARTS)], axis=0
@@ -363,6 +383,10 @@
 
     route_field(1)
 
+    @pl.when(s < slabs // 4)
+    def _():
+        share_all()
+
     route_field(2)
 
     rim_here = jnp.logical_or(
@@ -382,10 +406,6 @@
 
         wanted_rim(m)
         pltpu.make_async_copy(out_rim.at[m], state_out.at[rim_slot], own_sem.at[3]).start()
-
-    @pl.when(s < slabs // 4)
-    def _():
-        share_all()
 
     share_batch = batch(z_lik, z_lik, slabs // 2 - 1, ls.at[0], lr.at[0])
     share_batch.wait_recv()
@@ -450,7 +470,7 @@
 
 def finish_kernel(
     slabs, state_in, bed_in, lik_in, water_out, east_out, south_out, weight_out,
-    a, b, bed, lik, done, in_sem, out_sem,
+    a, b, bed, lik, done, weight, in_sem, out_sem,
 ):
     m = lax.axis_index("member")
     s = lax.axis_index("space")
@@ -497,7 +517,9 @@
     log_mass = jnp.log(jnp.broadcast_to(mass, rows.shape))
     for p in range(PARTS):
         weights = totals[p] - top - log_mass
-        weight_out[p] = jnp.sum(jnp.where(jnp.logical_and(own, once), weights, 0.0))
+        weight[p] = jnp.sum(jnp.where(jnp.logical_and(own, once), weights, 0.0))
+    copies.append(pltpu.make_async_copy(weight, weight_out, in_sem.at[4]))
+    copies[0].start()
     loads[0].wait()
     loads[1].wait()
     step_rows(a, bed, -1, half + 2, 5, first, last_row, keep_in(b, RIM))
@@ -528,7 +550,6 @@
     parts, rows, width = depth.shape
     f32 = jnp.float32
     hbm = pl.BlockSpec(memory_space=pl.ANY)
-    smem = pl.BlockSpec(memory_space=pltpu.SMEM)
     row = (PARTS, SUB, LANES)
     dma = pltpu.SemaphoreType.DMA
     steps = slabs.bit_length() - 1
@@ -586,14 +607,15 @@
         out_shape=(jax.ShapeDtypeStruct((cells, LANES), f32),) * 3
         + (jax.ShapeDtypeStruct((parts,), f32),),
         in_specs=[hbm] * 3,
-        out_specs=(hbm, hbm, hbm, smem),
+        out_specs=(hbm, hbm, hbm, hbm),
         scratch_shapes=[
             pltpu.VMEM((3 * EXT, *row), f32),
             pltpu.VMEM((3 * EXT, *row), f32),
             pltpu.VMEM((EXT, 2, SUB, LANES), f32),
             pltpu.VMEM((2 * members, 1, LANES), f32),
             pltpu.VMEM((3, cells, LANES), f32),
-            dma((4,)), dma((2, PARTS, 3)),
+            pltpu.SMEM((parts,), f32),
+            dma((5,)), dma((2, PARTS, 3)),
         ],
         compiler_params=pltpu.CompilerParams(vmem_limit_bytes=VMEM_LIMIT),
         name="finish",

time: 47.1 us -> 46 us (0.977)
  Pallas kernels: 46.2 us -> 45.1 us
    pallas_call x1, Pallas kernels: 41.7 us -> 41.1 us  [shards(): pl.pallas_call(functools.partial(exchange_kernel, members, slabs), out_sh...]
    pallas_call x1, Pallas kernels: 4.49 us -> 3.99 us  [shards(): pl.pallas_call(functools.partial(finish_kernel, slabs), out_shape=(jax.Sh...]
where the time goes in v5:
time: 46 us; the launch traced here: 45.8 us
  Pallas kernels  45.1 us (98%)
  between operations  0.64 us (1%)
    pallas_call x1, Pallas kernels, shards(): pl.pallas_call(functools.partial(exchange_kernel, members, slabs), out_sh...  41.1 us
    pallas_call x1, Pallas kernels, shards(): pl.pallas_call(functools.partial(finish_kernel, slabs), out_shape=(jax.Sh...  3.99 us

profile of v5, /device:TPU:1, one launch (start us, length us, event | category | flops | bytes accessed | tf_op | source)
XLA Modules:
  0.0 45.8 jit_solution(5378074715507034229)
XLA Ops:
  0.6 41.1 %exchange.1 = (f32[60,2,16,128]{3,2,1,0:T(8,128)}, f32[20,2,16,128]{3,2,1,0:T(8,128)}, f32[32,1,128]{2,1,0:T(1,128)}) custom-call(f32[512,128]{1,0:T(8,128)} %bitcast.42, f32[512,128]{1,0:T(8,128)} %bitcast.43, f32[512,128]{1,0:T(8,128)} %bitcast.44, f32[256,128]{1,0:T(8,128)} %bitcast.45, f32[256,128]{1,0:T(8,128)} %bitcast.46, s32[1,512]{1,0:T(1,128)} %bitcast.47, ...), custom_call_target="tpu_custom_call" | custom-call | tf_op jit(solution)/shard_map/exchange/pallas_call | solution.py:558
  41.8 4.0 %finish.1 = (f32[512,128]{1,0:T(8,128)}, f32[512,128]{1,0:T(8,128)}, f32[512,128]{1,0:T(8,128)}, f32[2]{0:T(128)}) custom-call(f32[60,2,16,128]{3,2,1,0:T(8,128)} %get-tuple-element.11.state_in, f32[20,2,16,128]{3,2,1,0:T(8,128)} %get-tuple-element.12.bed_in, f32[32,1,128]{2,1,0:T(1,128)} %get-tuple-element.13.lik_in), custom_call_target="tpu_custom_call" | custom-call | tf_op jit(solution)/shard_map/finish/pallas_call | solution.py:605

commit v6 on v5

--- a/solution.py
+++ b/solution.py
@@ -158,6 +158,14 @@
             greet(m, slab)
             greet(across, slab)
 
+    @pl.when(s >= 2)
+    def _():
+        greet(m, s - 2)
+
+    @pl.when(s + 2 < slabs)
+    def _():
+        greet(m, s + 2)
+
     @pl.loop(1, members)
     def _(i):
         greet(lax.rem(m + i, members), s)
@@ -179,7 +187,8 @@
         lay_out(r)
         lay_out(ROWS - 1 - r)
 
-    pl.semaphore_wait(barrier, members - 1 + 2 * (has_up + has_down))
+    two_away = (s + slabs - 2) // slabs + (2 * slabs - 3 - s) // slabs
+    pl.semaphore_wait(barrier, members - 1 + 2 * (has_up + has_down) + two_away)
 
     low, high = 3 * RIM, 3 * (RIM + ROWS)
     halos_down = [
@@ -219,7 +228,7 @@
         def _():
             pl.semaphore_wait(here_sem.at[2 * t + 1], 1)
 
-    announce(0)
+    announce(1)
 
     @pl.loop(RIM, ROWS - RIM)
     def _(r):
@@ -228,8 +237,8 @@
     step_rows(a, bed, 1, ROWS - 2, 7, first, last_row, keep_in(b, RIM))
     step_rows(b, bed, 2, ROWS - 4, 4, first, last_row, keep_in(c, 0))
 
-    heard(0)
-    announce(1)
+    heard(1)
+    announce(2)
 
     def spread(to, f):
         return remote(c.at[3 * to + f], held[f].at[m], s1.at[f], r1.at[f], to, s)
@@ -256,8 +265,6 @@
         lax.broadcasted_iota(jnp.int32, (LANES, count), 0) == lane, inside
     )
 
-    heard(1)
-    announce(2)
     def third():
         heard(2)
         announce(3)

time: 46 us -> 43.8 us (0.952)
  the two profiles are of different devices: /device:TPU:1 before, /device:TPU:325 now
where the time goes in v6:
time: 43.8 us; the launch traced here: 43.5 us
  Pallas kernels  42.9 us (98%)
  between operations  0.64 us (1%)
    pallas_call x1, Pallas kernels, shards(): pl.pallas_call(functools.partial(exchange_kernel, members, slabs), out_sh...  38.9 us
    pallas_call x1, Pallas kernels, shards(): pl.pallas_call(functools.partial(finish_kernel, slabs), out_shape=(jax.Sh...  3.99 us

profile of v6, /device:TPU:325, one launch (start us, length us, event | category | flops | bytes accessed | tf_op | source)
XLA Modules:
  0.0 43.5 jit_solution(9994716091520990437)
XLA Ops:
  0.6 38.9 %exchange.1 = (f32[60,2,16,128]{3,2,1,0:T(8,128)}, f32[20,2,16,128]{3,2,1,0:T(8,128)}, f32[32,1,128]{2,1,0:T(1,128)}) custom-call(f32[512,128]{1,0:T(8,128)} %bitcast.42, f32[512,128]{1,0:T(8,128)} %bitcast.43, f32[512,128]{1,0:T(8,128)} %bitcast.44, f32[256,128]{1,0:T(8,128)} %bitcast.45, f32[256,128]{1,0:T(8,128)} %bitcast.46, s32[1,512]{1,0:T(1,128)} %bitcast.47, ...), custom_call_target="tpu_custom_call" | custom-call | tf_op jit(solution)/shard_map/exchange/pallas_call | solution.py:565
  39.6 4.0 %finish.1 = (f32[512,128]{1,0:T(8,128)}, f32[512,128]{1,0:T(8,128)}, f32[512,128]{1,0:T(8,128)}, f32[2]{0:T(128)}) custom-call(f32[60,2,16,128]{3,2,1,0:T(8,128)} %get-tuple-element.11.state_in, f32[20,2,16,128]{3,2,1,0:T(8,128)} %get-tuple-element.12.bed_in, f32[32,1,128]{2,1,0:T(1,128)} %get-tuple-element.13.lik_in), custom_call_target="tpu_custom_call" | custom-call | tf_op jit(solution)/shard_map/finish/pallas_call | solution.py:612
